TPU v7x, 512 devices: a whole 4x4x16 slice. The times are simulated.
512 devices in a mesh: ctx: 64 (over x, z_hi, y, core), ch: 8 (over z_lo).
Axes of the slice: x: 4, y: 4, z: 16 (z_hi: 2, z_lo: 8; z = z_hi * 8 + z_lo), core: 2. Of those that a mesh axis runs over, the one named last changes fastest.
Arguments:
- queries: bfloat16 [256, 8192], P('ch', 'ctx'), may hold values from -6 to 6
- keys: bfloat16 [256, 8192], P('ch', 'ctx'), may hold values from -6 to 6
- values: bfloat16 [256, 8192], P('ch', 'ctx'), may hold values from -6 to 6
- upstream: bfloat16 [256, 8192], P('ch', 'ctx'), may hold values from -6 to 6
- residues: float32 [256, 16], P('ch'), may hold values from -3 to 3
- rates: float32 [256, 16], P('ch'), may hold values from 3.6621093e-06 to 0.05
- w_in: bfloat16 [3, 256, 8192], P(None, 'ch'), may hold values from -0.3125 to 0.3125
Outputs:
- grad_input: bfloat16 [8192, 8192], P('ch', 'ctx')
- grad_residues: float32 [256, 16], P('ch')
- grad_lograte: float32 [256, 16], P('ch')
All inputs are finite; a program needn't handle non-finite values.
Results may differ from a plain program's by a relative error of at most 0.017.
Values may be sent and summed in bfloat16 or wider, within the bound.
A program may use at most 64 MiB of HBM per device.

v0:
```python
import math

import jax
import jax.numpy as jnp
from jax import lax
from jax.sharding import PartitionSpec as P

HIGHEST_PRECISION = lax.Precision.HIGHEST


def angle_table(first, second, modulus):
    product = first[:, None] * second[None, :] % modulus
    return product.astype(jnp.float32) * (2.0 * math.pi / modulus)


def forward_transform(signal):
    ctx_count = lax.axis_size("ctx")
    local_len = signal.shape[1]
    piece_len = local_len // ctx_count
    total_len = 2 * ctx_count * local_len
    by_source = lax.all_to_all(signal[:, None, :], "ctx", split_axis=2, concat_axis=1, tiled=True)
    source_ids = jnp.arange(ctx_count, dtype=jnp.int32)
    coarse_ids = jnp.arange(2 * ctx_count, dtype=jnp.int32)
    coarse_angle = angle_table(source_ids, coarse_ids, 2 * ctx_count)
    real_part = jnp.einsum(
        "rpj,pk->rjk", by_source, jnp.cos(coarse_angle), precision=HIGHEST_PRECISION
    )
    imag_part = -jnp.einsum(
        "rpj,pk->rjk", by_source, jnp.sin(coarse_angle), precision=HIGHEST_PRECISION
    )
    fine_ids = lax.axis_index("ctx") * piece_len + jnp.arange(piece_len, dtype=jnp.int32)
    twiddle = angle_table(fine_ids, coarse_ids, total_len)
    cosine = jnp.cos(twiddle)
    sine = jnp.sin(twiddle)
    turned = jnp.stack(
        [real_part * cosine + imag_part * sine, imag_part * cosine - real_part * sine]
    )
    by_column = lax.all_to_all(turned, "ctx", split_axis=3, concat_axis=2, tiled=True)
    local_ids = jnp.arange(local_len, dtype=jnp.int32)
    fine_angle = angle_table(local_ids, local_ids, local_len)
    cos_fine = jnp.cos(fine_angle)
    sin_fine = jnp.sin(fine_angle)
    spec_real = jnp.einsum(
        "rjl,jk->rlk", by_column[0], cos_fine, precision=HIGHEST_PRECISION
    ) + jnp.einsum("rjl,jk->rlk", by_column[1], sin_fine, precision=HIGHEST_PRECISION)
    spec_imag = jnp.einsum(
        "rjl,jk->rlk", by_column[1], cos_fine, precision=HIGHEST_PRECISION
    ) - jnp.einsum("rjl,jk->rlk", by_column[0], sin_fine, precision=HIGHEST_PRECISION)
    return (spec_real, spec_imag)


def inverse_transform(spec_real, spec_imag):
    ctx_count = lax.axis_size("ctx")
    local_len = spec_real.shape[2]
    total_len = 2 * ctx_count * local_len
    local_ids = jnp.arange(local_len, dtype=jnp.int32)
    fine_angle = angle_table(local_ids, local_ids, local_len)
    cos_fine = jnp.cos(fine_angle)
    sin_fine = jnp.sin(fine_angle)
    wave_real = jnp.einsum(
        "rlk,jk->rlj", spec_real, cos_fine, precision=HIGHEST_PRECISION
    ) - jnp.einsum("rlk,jk->rlj", spec_imag, sin_fine, precision=HIGHEST_PRECISION)
    wave_imag = jnp.einsum(
        "rlk,jk->rlj", spec_imag, cos_fine, precision=HIGHEST_PRECISION
    ) + jnp.einsum("rlk,jk->rlj", spec_real, sin_fine, precision=HIGHEST_PRECISION)
    coarse_local = lax.axis_index("ctx") * 2 + jnp.arange(2, dtype=jnp.int32)
    twiddle = angle_table(coarse_local, local_ids, total_len)
    cosine = jnp.cos(twiddle)
    sine = jnp.sin(twiddle)
    turned = jnp.stack(
        [wave_real * cosine - wave_imag * sine, wave_imag * cosine + wave_real * sine]
    )
    by_piece = lax.all_to_all(turned, "ctx", split_axis=3, concat_axis=2, tiled=True)
    source_ids = jnp.arange(ctx_count, dtype=jnp.int32)
    coarse_ids = jnp.arange(2 * ctx_count, dtype=jnp.int32)
    coarse_angle = angle_table(coarse_ids, source_ids, 2 * ctx_count)
    samples = jnp.einsum(
        "rkj,km->rmj", by_piece[0], jnp.cos(coarse_angle), precision=HIGHEST_PRECISION
    ) - jnp.einsum("rkj,km->rmj", by_piece[1], jnp.sin(coarse_angle), precision=HIGHEST_PRECISION)
    samples = samples / float(total_len)
    restored = lax.all_to_all(samples, "ctx", split_axis=1, concat_axis=2, tiled=True)
    return restored[:, 0, :]


def per_device(queries, keys, values, upstream, residues, rates, w_in):
    local_len = queries.shape[1]
    chan_count = queries.shape[0]
    ctx_count = lax.axis_size("ctx")
    positions = (lax.axis_index("ctx") * local_len + jnp.arange(local_len, dtype=jnp.int32)).astype(
        jnp.float32
    )
    mode_gain = jnp.sqrt(2.0 * rates)
    decaying = jnp.exp(-rates[:, :, None] * positions[None, None, :])
    filter_taps = jnp.einsum(
        "cm,cmt->ct", residues * mode_gain, decaying, precision=HIGHEST_PRECISION
    )
    key_f = keys.astype(jnp.float32)
    value_f = values.astype(jnp.float32)
    mixed = key_f * value_f
    first_real, first_imag = forward_transform(jnp.concatenate([mixed, filter_taps], axis=0))
    mixed_real = first_real[:chan_count]
    mixed_imag = first_imag[:chan_count]
    filter_real = first_real[chan_count:]
    filter_imag = first_imag[chan_count:]
    conv = inverse_transform(
        filter_real * mixed_real - filter_imag * mixed_imag,
        filter_real * mixed_imag + filter_imag * mixed_real,
    )
    upstream_f = upstream.astype(jnp.float32)
    dgate = upstream_f * queries.astype(jnp.float32)
    dquery = upstream_f * conv
    grad_real, grad_imag = forward_transform(dgate)
    pair_real = jnp.concatenate(
        [
            filter_real * grad_real + filter_imag * grad_imag,
            mixed_real * grad_real + mixed_imag * grad_imag,
        ],
        axis=0,
    )
    pair_imag = jnp.concatenate(
        [
            filter_real * grad_imag - filter_imag * grad_real,
            mixed_real * grad_imag - mixed_imag * grad_real,
        ],
        axis=0,
    )
    both_grads = inverse_transform(pair_real, pair_imag)
    dmixed = both_grads[:chan_count]
    dfilter = both_grads[chan_count:]
    grad_stack = jnp.stack([dquery, dmixed * value_f, dmixed * key_f]).astype(jnp.bfloat16)
    residue_part = (
        jnp.einsum("ct,cmt->cm", dfilter, decaying, precision=HIGHEST_PRECISION) * mode_gain
    )
    ramp = 0.5 - rates[:, :, None] * positions[None, None, :]
    lograte_part = (
        residues
        * mode_gain
        * jnp.einsum("ct,cmt->cm", dfilter, decaying * ramp, precision=HIGHEST_PRECISION)
    )
    residue_total, lograte_total = lax.psum((residue_part, lograte_part), "ctx")
    scale = 1.0 / math.sqrt(float(local_len * ctx_count))
    summed = lax.psum_scatter(
        jnp.einsum("act,acd->dt", grad_stack, w_in, preferred_element_type=jnp.float32).astype(
            jnp.bfloat16
        ),
        "ch",
        scatter_dimension=0,
        tiled=True,
    )
    return (summed, residue_total * scale, lograte_total * scale)


def solution(mesh):
    return jax.shard_map(
        per_device,
        mesh=mesh,
        in_specs=(
            P("ch", "ctx"),
            P("ch", "ctx"),
            P("ch", "ctx"),
            P("ch", "ctx"),
            P("ch", None),
            P("ch", None),
            P(None, "ch", None),
        ),
        out_specs=(P("ch", "ctx"), P("ch", None), P("ch", None)),
        check_vma=False,
    )
```

profile of v0, /device:TPU:32, one launch (start us, length us, event | category | flops | bytes accessed | tf_op | source)
XLA Modules:
  0.0 789.0 jit_solution(2854483732847190395)
XLA Ops:
  7.2 0.8 fusion.87
  8.0 0.7 copy.80
  8.7 20.3 %all-to-all-start.4 = ((f32[32,1,128]{0,1,2:T(1,128)}), f32[32,1,128]{0,1,2:T(1,128)S(1)}, u32[]{:S(2)}, u32[]{:S(2)}) async-start(f32[32,1,128]{0,1,2:T(1,128)} %copy.80), calls=%async_computation.4 | async-start | bytes 131072 | tf_op jit(solution)/shard_map/all_to_all | solution.py:21
  29.2 0.7 fusion.220
  31.9 0.8 reduce.5
  33.4 12.4 %all-to-all-done.4 = f32[32,1,128]{0,1,2:T(1,128)S(1)} async-done(((f32[32,1,128]{0,1,2:T(1,128)}), f32[32,1,128]{0,1,2:T(1,128)S(1)}, u32[]{:S(2)}, u32[]{:S(2)}) %all-to-all-start.4) | async-done | bytes 16416 | tf_op jit(solution)/shard_map/all_to_all | solution.py:21
  45.8 5.2 all-to-all-start
  51.9 0.9 reshape.116
  52.8 14.9 %all-to-all-done = f32[64,1,128]{2,1,0:T(1,128)S(1)} async-done(((f32[64,1,128]{2,1,0:T(1,128)}), f32[64,1,128]{2,1,0:T(1,128)S(1)}, u32[]{:S(2)}, u32[]{:S(2)}) %all-to-all-start) | async-done | bytes 32800 | tf_op jit(solution)/shard_map/all_to_all | solution.py:21
  67.6 4.6 all-to-all-start.5
  74.1 0.9 reshape.120
  75.0 14.0 %all-to-all-done.5 = f32[64,1,256]{2,1,0:T(1,128)S(1)} async-done(((f32[64,1,256]{2,1,0:T(1,128)}), f32[64,1,256]{2,1,0:T(1,128)S(1)}, u32[]{:S(2)}, u32[]{:S(2)}) %all-to-all-start.5) | async-done | bytes 65568 | tf_op jit(solution)/shard_map/all_to_all | solution.py:38
  89.0 4.8 all-to-all-start.1
  93.8 0.8 reduce.4
  96.6 18.5 %all-to-all-done.1 = f32[64,1,512]{2,1,0:T(1,128)S(1)} async-done(((f32[64,1,512]{2,1,0:T(1,128)}), f32[64,1,512]{2,1,0:T(1,128)S(1)}, u32[]{:S(2)}, u32[]{:S(2)}) %all-to-all-start.1) | async-done | bytes 131104 | tf_op jit(solution)/shard_map/all_to_all | solution.py:38
  115.0 1.0 reduce.7
  121.0 0.9 reshape.126
  121.9 4.6 all-to-all-start.2
  128.5 15.7 %all-to-all-done.2 = f32[64,1,256]{2,1,0:T(1,128)S(1)} async-done(((f32[64,1,256]{2,1,0:T(1,128)}), f32[64,1,256]{2,1,0:T(1,128)S(1)}, u32[]{:S(2)}, u32[]{:S(2)}) %all-to-all-start.2) | async-done | bytes 65568 | tf_op jit(solution)/shard_map/all_to_all | solution.py:73
  144.2 0.8 reduce.10
  147.0 4.6 all-to-all-start.3
  151.8 0.9 reshape.122
  152.8 17.0 %all-to-all-done.3 = f32[32,64,2]{0,2,1:T(2,128)S(1)} async-done(((f32[32,64,2]{0,2,1:T(2,128)}), f32[32,64,2]{0,2,1:T(2,128)S(1)}, u32[]{:S(2)}, u32[]{:S(2)}) %all-to-all-start.3) | async-done | bytes 16416 | tf_op jit(solution)/shard_map/all_to_all | solution.py:81
  169.8 4.8 all-to-all-start.6
  174.7 20.1 %all-to-all-done.6 = f32[64,1,512]{2,1,0:T(1,128)S(1)} async-done(((f32[64,1,512]{2,1,0:T(1,128)}), f32[64,1,512]{2,1,0:T(1,128)S(1)}, u32[]{:S(2)}, u32[]{:S(2)}) %all-to-all-start.6) | async-done | bytes 131104 | tf_op jit(solution)/shard_map/all_to_all | solution.py:73
  194.7 1.0 reduce.8
  197.0 0.7 reshape.124
  197.7 4.6 all-to-all-start.7
  202.4 16.5 %all-to-all-done.7 = f32[64,1,128]{2,1,0:T(1,128)S(1)} async-done(((f32[64,1,128]{2,1,0:T(1,128)}), f32[64,1,128]{2,1,0:T(1,128)S(1)}, u32[]{:S(2)}, u32[]{:S(2)}) %all-to-all-start.7) | async-done | bytes 32800 | tf_op jit(solution)/shard_map/all_to_all | solution.py:81
  220.0 2.1 fusion.1
  223.4 556.4 %all-reduce = (f32[32,16]{0,1:T(8,128)S(1)}, f32[32,16]{0,1:T(8,128)S(1)}) all-reduce(f32[32,16]{0,1:T(8,128)S(1)} %get-tuple-element.43, f32[32,16]{0,1:T(8,128)S(1)} %get-tuple-element.42), channel_id=1, replica_groups=mesh['ctx'=64,'ch'=8] {'ctx'}, use_global_device_ids=true, to_apply=%region_1.2 | all-reduce | flops 1024 | bytes 8192 | tf_op jit(solution)/shard_map/psum | solution.py:140
  780.4 1.8 copy.101
  (98 shorter events, 20.6 us)
Async XLA Ops:
  7.2 212.8 %copy-start = (bf16[3,32,8192]{2,1,0:T(8,128)(2,1)S(1)}, bf16[3,32,8192]{2,1,0:T(8,128)(2,1)}, u32[]{:S(2)}) copy-start(bf16[3,32,8192]{2,1,0:T(8,128)(2,1)} %param.13) | copy-start | bytes 4718596
  8.7 37.0 %all-to-all-start.4 = ((f32[32,1,128]{0,1,2:T(1,128)}), f32[32,1,128]{0,1,2:T(1,128)S(1)}, u32[]{:S(2)}, u32[]{:S(2)}) async-start(f32[32,1,128]{0,1,2:T(1,128)} %copy.80), calls=%async_computation.4 | async-start | bytes 131072 | tf_op jit(solution)/shard_map/all_to_all | solution.py:21
  45.8 21.9 %all-to-all-start = ((f32[64,1,128]{2,1,0:T(1,128)}), f32[64,1,128]{2,1,0:T(1,128)S(1)}, u32[]{:S(2)}, u32[]{:S(2)}) async-start(f32[64,1,128]{2,1,0:T(1,128)} %reshape.118), calls=%async_computation | async-start | bytes 65536 | tf_op jit(solution)/shard_map/all_to_all | solution.py:21
  67.6 21.3 %all-to-all-start.5 = ((f32[64,1,256]{2,1,0:T(1,128)}), f32[64,1,256]{2,1,0:T(1,128)S(1)}, u32[]{:S(2)}, u32[]{:S(2)}) async-start(f32[64,1,256]{2,1,0:T(1,128)} %reshape.116), calls=%async_computation.5 | async-start | bytes 131072 | tf_op jit(solution)/shard_map/all_to_all | solution.py:38
  89.0 26.0 %all-to-all-start.1 = ((f32[64,1,512]{2,1,0:T(1,128)}), f32[64,1,512]{2,1,0:T(1,128)S(1)}, u32[]{:S(2)}, u32[]{:S(2)}) async-start(f32[64,1,512]{2,1,0:T(1,128)} %reshape.120), calls=%async_computation.1 | async-start | bytes 262144 | tf_op jit(solution)/shard_map/all_to_all | solution.py:38
  121.9 22.4 %all-to-all-start.2 = ((f32[64,1,256]{2,1,0:T(1,128)}), f32[64,1,256]{2,1,0:T(1,128)S(1)}, u32[]{:S(2)}, u32[]{:S(2)}) async-start(f32[64,1,256]{2,1,0:T(1,128)} %reshape.126), calls=%async_computation.2 | async-start | bytes 131072 | tf_op jit(solution)/shard_map/all_to_all | solution.py:73
  147.0 22.7 %all-to-all-start.3 = ((f32[32,64,2]{0,2,1:T(2,128)}), f32[32,64,2]{0,2,1:T(2,128)S(1)}, u32[]{:S(2)}, u32[]{:S(2)}) async-start(f32[32,64,2]{0,2,1:T(2,128)} %copy.78), calls=%async_computation.3 | async-start | bytes 131072 | tf_op jit(solution)/shard_map/all_to_all | solution.py:81
  169.8 25.0 %all-to-all-start.6 = ((f32[64,1,512]{2,1,0:T(1,128)}), f32[64,1,512]{2,1,0:T(1,128)S(1)}, u32[]{:S(2)}, u32[]{:S(2)}) async-start(f32[64,1,512]{2,1,0:T(1,128)} %reshape.122), calls=%async_computation.6 | async-start | bytes 262144 | tf_op jit(solution)/shard_map/all_to_all | solution.py:73
  174.6 27.7 %copy-start.2 = (bf16[32,128]{1,0:T(8,128)(2,1)S(1)}, bf16[32,128]{1,0:T(8,128)(2,1)}, u32[]{:S(2)}) copy-start(bf16[32,128]{1,0:T(8,128)(2,1)} %param.10) | copy-start | bytes 24580
  195.7 24.2 %copy-start.3 = (bf16[32,128]{1,0:T(8,128)(2,1)S(1)}, bf16[32,128]{1,0:T(8,128)(2,1)}, u32[]{:S(2)}) copy-start(bf16[32,128]{1,0:T(8,128)(2,1)} %param.9) | copy-start | bytes 24580
  195.7 24.2 %copy-start.4 = (bf16[32,128]{1,0:T(8,128)(2,1)S(1)}, bf16[32,128]{1,0:T(8,128)(2,1)}, u32[]{:S(2)}) copy-start(bf16[32,128]{1,0:T(8,128)(2,1)} %param.8) | copy-start | bytes 24580
  197.7 21.2 %all-to-all-start.7 = ((f32[64,1,128]{2,1,0:T(1,128)}), f32[64,1,128]{2,1,0:T(1,128)S(1)}, u32[]{:S(2)}, u32[]{:S(2)}) async-start(f32[64,1,128]{2,1,0:T(1,128)} %reshape.124), calls=%async_computation.7 | async-start | bytes 65536 | tf_op jit(solution)/shard_map/all_to_all | solution.py:81
  202.3 578.1 %reduce-scatter.2.cloned.1.call-start = ((), (), s32[]{:S(2)}) async-start(), calls=%async_computation.9 | async-start | bytes 2359296 | tf_op jit(solution)/shard_map/reduce_scatter | solution.py:142
  222.1 0.7 copy-start.1
  222.1 1.3 copy-start.5
Sparse Core Ops, SparseCore 0:
  222.2 56.6 reduce-scatter.1
where the time goes:
time: 790 us; the launch traced here: 789 us
  blocking collectives  556 us (70%)
  waiting for transfers between devices  129 us (16%)
  starting transfers between devices  53.5 us (7%)
  between operations  14.7 us (2%)
  local copies, waits for them, and re-layouts  13.3 us (2%)
  matrix products  12.9 us (2%)
  other arithmetic  9.22 us (1%)
    psum x1, blocking collectives, per_device(): residue_total, lograte_total = lax.psum((residue_part, lograte_part), 'ctx')  556 us
    all_to_all x2, waiting for transfers between devices, inverse_transform(): lax.all_to_all(turned, 'ctx', split_axis=3, concat_axis=2, tiled=True)  35.8 us
    all_to_all x2, waiting for transfers between devices, inverse_transform(): lax.all_to_all(samples, 'ctx', split_axis=1, concat_axis=2, tiled=True)  33.6 us
    all_to_all x2, waiting for transfers between devices, forward_transform(): lax.all_to_all(turned, 'ctx', split_axis=3, concat_axis=2, tiled=True)  32.4 us
    all_to_all x2, waiting for transfers between devices, forward_transform(): lax.all_to_all(signal[:, None, :], 'ctx', split_axis=2, concat_axis=1, ti...  27.3 us
    all_to_all x2, starting transfers between devices, forward_transform(): lax.all_to_all(signal[:, None, :], 'ctx', split_axis=2, concat_axis=1, ti...  25.4 us
  transfers between devices with their start and end apart: 9, of which 8 were waited for; matrix products, arithmetic and copies ran while one was open for 2% of the time, Pallas kernels for 0%

commit v1 on v0

v1 whole, which is shorter than its diff:
```python
import functools
import math

import jax
import jax.numpy as jnp
from jax import lax
from jax.experimental import pallas as pl
from jax.experimental.pallas import tpu as pltpu
from jax.sharding import PartitionSpec as P

MESH = pl.DeviceIdType.MESH
HIGHEST = lax.Precision.HIGHEST
F32 = jnp.float32
LANES = 128
HALF = 16


def dot(lhs, rhs, dims=((1,), (0,)), precision=HIGHEST):
    return lax.dot_general(
        lhs, rhs, (dims, ((), ())), precision=precision, preferred_element_type=F32
    )


def dot_nt(lhs, rhs):
    return dot(lhs, rhs, ((1,), (1,)))


def iota(shape, dim):
    return lax.broadcasted_iota(jnp.int32, shape, dim)


def one_where(condition):
    return jnp.where(condition, 1.0, 0.0).astype(F32)


def kernel(
    dims,
    token_count,
    q_ref,
    k_ref,
    v_ref,
    u_ref,
    res_ref,
    rate_ref,
    w_ref,
    out_ref,
    gres_ref,
    glog_ref,
    near_buf,
    far_buf,
    near_sum,
    far_sum,
    dz_buf,
    w_buf,
    own_sem,
    near_send,
    near_recv,
    far_send,
    far_recv,
    nsum_send,
    nsum_recv,
    fsum_send,
    fsum_recv,
    dz_send,
    dz_recv,
    wz_send,
    wz_recv,
    wx_send,
    wx_recv,
    wc_send,
    wc_recv,
):
    nx, nzh, ny, nco, nzl = dims
    nb, na = ny * nco, nx * nzh
    nz = nzh * nzl
    ctx = lax.axis_index("ctx")
    zlo = lax.axis_index("ch")
    near = lax.rem(ctx, nb)
    far = ctx // nb
    core = lax.rem(ctx, nco)
    y = near // nco
    zh = lax.rem(far, nzh)
    x = far // nzh
    z = zh * nzl + zlo
    chans, span = q_ref.shape
    modes = res_ref.shape[1]
    pairs = chans * modes
    blocks = pairs // LANES
    d_len = w_buf.shape[3]

    def ctx_of(px, pzh, py, pco):
        return ((px * nzh + pzh) * ny + py) * nco + pco

    def near_peer(step):
        return {"ctx": far * nb + lax.rem(near + step, nb), "ch": zlo}

    def far_peer(step):
        return {"ctx": lax.rem(far + step, na) * nb + near, "ch": zlo}

    def line_peer(step):
        return {"ctx": ctx, "ch": lax.rem(zlo + step, nzl)}

    def ring_peer(step):
        there = lax.rem(z + step + nz, nz)
        return {"ctx": ctx_of(x, there // nzl, y, core), "ch": lax.rem(there, nzl)}

    def x_peer(step):
        return {"ctx": ctx_of(lax.rem(x + step, nx), zh, y, core), "ch": zlo}

    def y_peer(step):
        return {"ctx": ctx_of(x, zh, lax.rem(y + step, ny), core), "ch": zlo}

    sibling = {"ctx": ctx_of(x, zh, y, lax.rem(core + 1, nco)), "ch": zlo}

    barrier = pltpu.get_barrier_semaphore()
    greeted = 0
    for peer_of, count in ((near_peer, nb), (far_peer, na), (ring_peer, nz)):
        for step in range(1, count):
            pl.semaphore_signal(barrier, inc=1, device_id=peer_of(step), device_id_type=MESH)
            greeted += 1

    own_copy = pltpu.make_async_copy(
        w_ref.at[:, :, pl.ds(pl.multiple_of(zlo * d_len, LANES), d_len)], w_buf.at[0], own_sem
    )
    own_copy.start()

    rates = rate_ref[...]
    gain = jnp.sqrt(2.0 * rates)
    weight = res_ref[...] * gain
    row_chan = one_where(iota((pairs, chans), 0) // modes == iota((pairs, chans), 1))
    row_mode = one_where(lax.rem(iota((pairs, modes), 0), modes) == iota((pairs, modes), 1))
    rate_rows = dot(dot(row_chan, rates) * row_mode, jnp.ones((modes, LANES), F32))
    lane_mode = one_where(iota((modes, pairs), 0) == lax.rem(iota((modes, pairs), 1), modes))
    lane_chan = one_where(iota((chans, pairs), 0) == iota((chans, pairs), 1) // modes)
    spread = dot(jnp.concatenate([rates, weight], axis=0), lane_mode)
    rate_lane = jnp.sum(spread[:chans] * lane_chan, axis=0, keepdims=True)
    weight_diag = spread[chans:] * lane_chan

    def folded(row):
        return [row[:, LANES * i : LANES * (i + 1)] for i in range(blocks)]

    rate4 = jnp.concatenate(folded(rate_lane), axis=0)
    rate8 = jnp.concatenate([rate4, rate4], axis=0)

    time = iota((pairs, span), 1).astype(F32)
    falling = jnp.exp(-rate_rows * time)
    rising = jnp.exp(rate_rows * time)
    chunk_decay = jnp.exp(-float(span) * rate_lane)
    chunk_decay4 = jnp.exp(-float(span) * rate4)

    value_f = v_ref[...].astype(F32)
    key_f = k_ref[...].astype(F32)
    up_f = u_ref[...].astype(F32)
    mixed = key_f * value_f
    dgate = up_f * q_ref[...].astype(F32)

    def diagonal_rows(full):
        return jnp.sum(full * lane_chan, axis=0, keepdims=True)

    steps = iota((chans, span), 1).astype(F32)
    from_mixed = dot_nt(jnp.concatenate([mixed, mixed * (float(span) - steps)], axis=0), rising)
    from_dgate = dot_nt(jnp.concatenate([dgate, dgate * steps], axis=0), falling)
    head = folded(diagonal_rows(from_mixed[:chans]) * chunk_decay) + folded(
        diagonal_rows(from_dgate[:chans])
    )
    state = jnp.concatenate(head, axis=0)
    near_buf[0] = state

    pl.semaphore_wait(barrier, greeted)

    def exchange(buf, send, recv, peer_of, count):
        copies = []
        for step in range(1, count):
            copies.append(
                pltpu.make_async_remote_copy(
                    src_ref=buf.at[0],
                    dst_ref=buf.at[step],
                    send_sem=send.at[step - 1],
                    recv_sem=recv.at[step - 1],
                    device_id=peer_of(step),
                    device_id_type=MESH,
                )
            )
        for copy in copies:
            copy.start()
        return copies

    near_copies = exchange(near_buf, near_send, near_recv, near_peer, nb)

    def half_view(slot, half, column):
        return w_buf.at[
            slot,
            :,
            pl.ds(half * HALF, HALF),
            pl.ds(pl.multiple_of(column * LANES, LANES), LANES),
        ]

    x_column = x * nco + core
    y_column = y * nco + core
    wz_copies = []
    for step in range(1, nzl):
        for half, column in ((0, x_column), (1, y_column)):
            hop = step if step < nzl // 2 + (1 - half) else step - nzl
            peer = ring_peer(hop)
            sem = 2 * (step - 1) + half
            wz_copies.append(
                pltpu.make_async_remote_copy(
                    src_ref=w_ref.at[
                        :,
                        pl.ds(half * HALF, HALF),
                        pl.ds(
                            pl.multiple_of(peer["ch"] * d_len + column * LANES, LANES), LANES
                        ),
                    ],
                    dst_ref=half_view(step, half, column),
                    send_sem=wz_send.at[sem],
                    recv_sem=wz_recv.at[sem],
                    device_id=peer,
                    device_id_type=MESH,
                )
            )
    for copy in wz_copies:
        copy.start()

    def over_modes(values):
        return jnp.broadcast_to(values[:, None, :], (chans, modes, span)).reshape(pairs, span)

    mixed_rows = over_modes(mixed)
    dgate_rows = over_modes(dgate)
    upper = one_where(iota((span, span), 0) <= iota((span, span), 1))
    lower = one_where(iota((span, span), 0) >= iota((span, span), 1))
    forward = falling * dot(rising * mixed_rows, upper)
    backward = rising * dot(falling * dgate_rows, lower)
    conv = dot(weight_diag, forward)
    dmixed = dot(weight_diag, backward)

    is_state = iota((2 * blocks, LANES), 0) < blocks

    def decay(length, if_state, if_other):
        steps_away = jnp.where(is_state, if_state, if_other).astype(F32)
        power = jnp.exp(-float(length) * rate8 * jnp.maximum(steps_away, 0.0))
        return jnp.where(steps_away >= 0.0, power, 0.0)

    before_near, whole_near = [], []
    for step in range(nb):
        other = lax.rem(near - step + nb, nb)
        before_near.append(decay(span, near - 1 - other, other - near - 1))
        whole_near.append(decay(span, nb - 1 - other, other))
    before_far = []
    for step in range(na):
        other = lax.rem(far - step + na, na)
        before_far.append(decay(span * nb, far - 1 - other, other - far - 1))
    inside = decay(span, near, nb - 1 - near)

    for copy in near_copies:
        copy.wait_recv()
    near_total = jnp.zeros_like(state)
    group = jnp.zeros_like(state)
    for step in range(nb):
        arrived = near_buf[step]
        near_total = near_total + before_near[step] * arrived
        group = group + whole_near[step] * arrived
    far_buf[0] = group
    far_copies = exchange(far_buf, far_send, far_recv, far_peer, na)

    for copy in wz_copies:
        copy.wait_recv()

    def column_view(half, column):
        return w_buf.at[
            pl.ds(1, nzl - 1),
            :,
            pl.ds(half * HALF, HALF),
            pl.ds(pl.multiple_of(column * LANES, LANES), LANES),
        ]

    def column_copy(half, column, send, recv, peer):
        view = column_view(half, column)
        return pltpu.make_async_remote_copy(
            src_ref=view,
            dst_ref=view,
            send_sem=send,
            recv_sem=recv,
            device_id=peer,
            device_id_type=MESH,
        )

    wx_copies, wc_copies = [], []
    for half, count, peer_of, column in ((0, nx, x_peer, x_column), (1, ny, y_peer, y_column)):
        for step in range(1, count):
            sem = half * (nx - 1) + step - 1
            wx_copies.append(
                column_copy(half, column, wx_send.at[sem], wx_recv.at[sem], peer_of(step))
            )
            wx_copies[-1].start()
    for half, column in ((0, x_column), (1, y_column)):
        wc_copies.append(column_copy(half, column, wc_send.at[half], wc_recv.at[half], sibling))
        wc_copies[-1].start()

    def lane_sums(rows):
        return dot_nt(jnp.ones((8, span), F32), rows)[0:1]

    same4 = jnp.concatenate(folded(diagonal_rows(dot_nt(dgate, forward))), axis=0)
    apart4 = jnp.concatenate(
        folded(lane_sums((forward - mixed_rows) * backward)), axis=0
    )
    ramp_s4 = jnp.concatenate(
        folded(diagonal_rows(from_mixed[chans:]) * chunk_decay), axis=0
    )
    ramp_g4 = jnp.concatenate(folded(diagonal_rows(from_dgate[chans:])), axis=0)
    s4, g4 = state[:blocks], state[blocks:]

    for copy in far_copies:
        copy.wait_recv()
    far_total = jnp.zeros_like(state)
    for step in range(na):
        far_total = far_total + before_far[step] * far_buf[step]
    entering = near_total + inside * far_total
    before4, after4 = entering[:blocks], entering[blocks:]

    def on_diagonal(rows):
        return weight_diag * jnp.concatenate([rows[i : i + 1] for i in range(blocks)], axis=1)

    conv = conv + dot(on_diagonal(before4), falling)
    dmixed = dmixed + dot(on_diagonal(after4 * chunk_decay4), rising)
    dz_buf[0, 0] = (up_f * conv).astype(jnp.bfloat16)
    dz_buf[0, 1] = (dmixed * value_f).astype(jnp.bfloat16)
    dz_buf[0, 2] = (dmixed * key_f).astype(jnp.bfloat16)
    dz_copies = exchange(dz_buf, dz_send, dz_recv, line_peer, nzl)

    same4 = same4 + g4 * before4
    apart4 = (
        apart4
        + before4 * (ramp_g4 + g4)
        + after4 * (ramp_s4 - s4)
        + float(span) * chunk_decay4 * before4 * after4
    )
    near_sum[0] = jnp.concatenate([same4, apart4], axis=0)
    nsum_copies = exchange(near_sum, nsum_send, nsum_recv, near_peer, nb)

    index = 0
    for half, count, place, base in ((0, nx, x, 0), (1, ny, y, nx - 1)):
        for step in range(1, count):
            wx_copies[index].wait_recv()
            column = lax.rem(place - step + count, count) * nco + core
            sem = 2 + base + step - 1
            wc_copies.append(column_copy(half, column, wc_send.at[sem], wc_recv.at[sem], sibling))
            wc_copies[-1].start()
            index += 1

    for copy in nsum_copies:
        copy.wait_recv()
    total = near_sum[0]
    for step in range(1, nb):
        total = total + near_sum[step]
    far_sum[0] = total
    fsum_copies = exchange(far_sum, fsum_send, fsum_recv, far_peer, na)

    own_copy.wait()
    for copy in wc_copies:
        copy.wait_recv()
    for copy in dz_copies:
        copy.wait_recv()
    rows = nzl * 3 * chans
    product = dot(
        dz_buf[...].reshape(rows, span), w_buf[...].reshape(rows, d_len), ((0,), (0,)), None
    )
    out_ref[...] = product.T.astype(jnp.bfloat16)

    for copy in fsum_copies:
        copy.wait_recv()
    total = far_sum[0]
    for step in range(1, na):
        total = total + far_sum[step]

    def unfolded(rows4):
        row = jnp.concatenate([rows4[i : i + 1] for i in range(blocks)], axis=1)
        return lane_chan * row

    sums = dot_nt(
        jnp.concatenate([unfolded(total[:blocks]), unfolded(total[blocks:])], axis=0), lane_mode
    )
    same, apart = sums[:chans], sums[chans:]
    scale = 1.0 / math.sqrt(float(token_count))
    gres_ref[...] = same * gain * scale
    glog_ref[...] = weight * (0.5 * same - rates * apart) * scale

    for copies in (
        near_copies,
        far_copies,
        wz_copies,
        wx_copies,
        wc_copies,
        dz_copies,
        nsum_copies,
        fsum_copies,
    ):
        for copy in copies:
            copy.wait_send()


def per_device(dims, queries, keys, values, upstream, residues, rates, w_in):
    nx, nzh, ny, nco, nzl = dims
    nb, na = ny * nco, nx * nzh
    chans, span = queries.shape
    modes = residues.shape[1]
    d_len = w_in.shape[2] // nzl
    fold = (2 * chans * modes // LANES, LANES)
    vmem = pl.BlockSpec(memory_space=pltpu.VMEM)
    dma = pltpu.SemaphoreType.DMA
    return pl.pallas_call(
        functools.partial(kernel, dims, span * na * nb),
        out_shape=(
            jax.ShapeDtypeStruct((d_len, span), jnp.bfloat16),
            jax.ShapeDtypeStruct((chans, modes), F32),
            jax.ShapeDtypeStruct((chans, modes), F32),
        ),
        in_specs=[vmem] * 6 + [pl.BlockSpec(memory_space=pl.ANY)],
        out_specs=(vmem, vmem, vmem),
        scratch_shapes=[
            pltpu.VMEM((nb,) + fold, F32),
            pltpu.VMEM((na,) + fold, F32),
            pltpu.VMEM((nb,) + fold, F32),
            pltpu.VMEM((na,) + fold, F32),
            pltpu.VMEM((nzl, 3, chans, span), jnp.bfloat16),
            pltpu.VMEM((nzl, 3, chans, d_len), jnp.bfloat16),
            dma,
            dma((nb - 1,)),
            dma((nb - 1,)),
            dma((na - 1,)),
            dma((na - 1,)),
            dma((nb - 1,)),
            dma((nb - 1,)),
            dma((na - 1,)),
            dma((na - 1,)),
            dma((nzl - 1,)),
            dma((nzl - 1,)),
            dma((2 * (nzl - 1),)),
            dma((2 * (nzl - 1),)),
            dma((nx + ny - 2,)),
            dma((nx + ny - 2,)),
            dma((nx + ny,)),
            dma((nx + ny,)),
        ],
        compiler_params=pltpu.CompilerParams(
            collective_id=0, has_side_effects=True, vmem_limit_bytes=40 * 1024 * 1024
        ),
        cost_estimate=pl.CostEstimate(
            flops=2 * 3 * chans * nzl * d_len * span, bytes_accessed=2 * w_in.size, transcendentals=0
        ),
    )(queries, keys, values, upstream, residues, rates, w_in)


def solution(mesh, dims=(4, 2, 4, 2, 8)):
    return jax.shard_map(
        functools.partial(per_device, dims),
        mesh=mesh,
        in_specs=(
            P("ch", "ctx"),
            P("ch", "ctx"),
            P("ch", "ctx"),
            P("ch", "ctx"),
            P("ch", None),
            P("ch", None),
            P(None, "ch", None),
        ),
        out_specs=(P("ch", "ctx"), P("ch", None), P("ch", None)),
        check_vma=False,
    )
```

time: 790 us -> 55.9 us (0.07)
  the two profiles are of different devices: /device:TPU:32 before, /device:TPU:64 now
where the time goes in v1:
time: 55.9 us; the launch traced here: 55.4 us
  Pallas kernels  47 us (84%)
  local copies, waits for them, and re-layouts  7.78 us (14%)
  between operations  0.65 us (1%)
    pallas_call x1, Pallas kernels, per_device(): pl.pallas_call(functools.partial(kernel, dims, span * na * nb), out_shape...  47 us
    unnamed x13, local copies, waits for them, and re-layouts  6.44 us
    pallas_call x2, local copies, waits for them, and re-layouts, per_device(): pl.pallas_call(functools.partial(kernel, dims, span * na * nb), out_shape...  1.34 us

profile of v1, /device:TPU:64, one launch (start us, length us, event | category | flops | bytes accessed | tf_op | source)
XLA Modules:
  0.0 55.4 jit_solution(8762578428713841734)
XLA Ops:
  0.6 0.8 %copy.10.res_ref = f32[32,16]{1,0:T(8,128)S(1)} copy(f32[32,16]{0,1:T(8,128)} %param.11) | data formatting | bytes 4096 | tf_op args[4]
  1.4 0.8 %copy.11.rate_ref = f32[32,16]{1,0:T(8,128)S(1)} copy(f32[32,16]{0,1:T(8,128)} %param.12) | data formatting | bytes 4096 | tf_op args[5]
  2.2 0.0 copy-start
  2.2 1.4 %copy-done = bf16[3,32,8192]{2,1,0:T(8,128)(2,1)S(1)} copy-done((bf16[3,32,8192]{2,1,0:T(8,128)(2,1)S(1)}, bf16[3,32,8192]{2,1,0:T(8,128)(2,1)}, u32[]{:S(2)}) %copy-start) | copy-done | bytes 1572888
  3.6 0.0 copy-start.1
  3.6 0.7 %copy-done.1 = bf16[32,128]{1,0:T(8,128)(2,1)S(1)} copy-done((bf16[32,128]{1,0:T(8,128)(2,1)S(1)}, bf16[32,128]{1,0:T(8,128)(2,1)}, u32[]{:S(2)}) %copy-start.1) | copy-done | bytes 8216
  4.3 0.0 copy-start.2
  4.3 0.7 %copy-done.2 = bf16[32,128]{1,0:T(8,128)(2,1)S(1)} copy-done((bf16[32,128]{1,0:T(8,128)(2,1)S(1)}, bf16[32,128]{1,0:T(8,128)(2,1)}, u32[]{:S(2)}) %copy-start.2) | copy-done | bytes 8216
  5.0 0.0 copy-start.3
  5.0 0.7 %copy-done.3 = bf16[32,128]{1,0:T(8,128)(2,1)S(1)} copy-done((bf16[32,128]{1,0:T(8,128)(2,1)S(1)}, bf16[32,128]{1,0:T(8,128)(2,1)}, u32[]{:S(2)}) %copy-start.3) | copy-done | bytes 8216
  5.7 0.0 copy-start.4
  5.7 0.7 %copy-done.4 = bf16[32,128]{1,0:T(8,128)(2,1)S(1)} copy-done((bf16[32,128]{1,0:T(8,128)(2,1)S(1)}, bf16[32,128]{1,0:T(8,128)(2,1)}, u32[]{:S(2)}) %copy-start.4) | copy-done | bytes 8216
  6.4 47.0 %shard_map.94 = (bf16[1024,128]{1,0:T(8,128)(2,1)S(1)}, f32[32,16]{1,0:T(8,128)S(1)}, f32[32,16]{1,0:T(8,128)S(1)}) custom-call(bf16[32,128]{1,0:T(8,128)(2,1)S(1)} %copy-done.1, bf16[32,128]{1,0:T(8,128)(2,1)S(1)} %copy-done.2, bf16[32,128]{1,0:T(8,128)(2,1)S(1)} %copy-done.3, bf16[32,128]{1,0:T(8,128)(2,1)S(1)} %copy-done.4, f32[32,16]{1,0:T(8,128)S(1)} %copy.10.res_ref, ...), custom_call_target="tpu_custom_call" | custom-call | flops 201326592 | bytes 1572864 | tf_op jit(solution)/shard_map/pallas_call | solution.py:411
  53.4 0.7 %copy.12 = f32[32,16]{0,1:T(8,128)} copy(f32[32,16]{1,0:T(8,128)S(1)} %get-tuple-element.4) | data formatting | bytes 4096 | tf_op jit(solution)/shard_map/pallas_call | solution.py:411
  54.1 0.7 %copy.13 = f32[32,16]{0,1:T(8,128)} copy(f32[32,16]{1,0:T(8,128)S(1)} %get-tuple-element.5) | data formatting | bytes 4096 | tf_op jit(solution)/shard_map/pallas_call | solution.py:411
  54.7 0.7 %copy.15 = bf16[1024,128]{1,0:T(8,128)(2,1)} copy(bf16[1024,128]{1,0:T(8,128)(2,1)S(1)} %get-tuple-element.9) | data formatting | bytes 524288
Async XLA Ops:
  2.2 1.4 %copy-start = (bf16[3,32,8192]{2,1,0:T(8,128)(2,1)S(1)}, bf16[3,32,8192]{2,1,0:T(8,128)(2,1)}, u32[]{:S(2)}) copy-start(bf16[3,32,8192]{2,1,0:T(8,128)(2,1)} %w_ref.1) | copy-start | bytes 4718596
  3.6 0.7 %copy-start.1 = (bf16[32,128]{1,0:T(8,128)(2,1)S(1)}, bf16[32,128]{1,0:T(8,128)(2,1)}, u32[]{:S(2)}) copy-start(bf16[32,128]{1,0:T(8,128)(2,1)} %q_ref.1) | copy-start | bytes 24580
  4.3 0.7 %copy-start.2 = (bf16[32,128]{1,0:T(8,128)(2,1)S(1)}, bf16[32,128]{1,0:T(8,128)(2,1)}, u32[]{:S(2)}) copy-start(bf16[32,128]{1,0:T(8,128)(2,1)} %k_ref.1) | copy-start | bytes 24580
  5.0 0.7 %copy-start.3 = (bf16[32,128]{1,0:T(8,128)(2,1)S(1)}, bf16[32,128]{1,0:T(8,128)(2,1)}, u32[]{:S(2)}) copy-start(bf16[32,128]{1,0:T(8,128)(2,1)} %v_ref.1) | copy-start | bytes 24580
  5.7 0.7 %copy-start.4 = (bf16[32,128]{1,0:T(8,128)(2,1)S(1)}, bf16[32,128]{1,0:T(8,128)(2,1)}, u32[]{:S(2)}) copy-start(bf16[32,128]{1,0:T(8,128)(2,1)} %u_ref.1) | copy-start | bytes 24580

commit v2 on v1

v2 whole, which is shorter than its diff:
```python
import functools
import math

import jax
import jax.numpy as jnp
from jax import lax
from jax.experimental import pallas as pl
from jax.experimental.pallas import tpu as pltpu
from jax.sharding import PartitionSpec as P

MESH = pl.DeviceIdType.MESH
HIGHEST = lax.Precision.HIGHEST
F32 = jnp.float32
LANES = 128
HALF = 16


def dot(lhs, rhs, dims=((1,), (0,)), precision=HIGHEST):
    return lax.dot_general(
        lhs, rhs, (dims, ((), ())), precision=precision, preferred_element_type=F32
    )


def dot_nt(lhs, rhs):
    return dot(lhs, rhs, ((1,), (1,)))


def iota(shape, dim):
    return lax.broadcasted_iota(jnp.int32, shape, dim)


def one_where(condition):
    return jnp.where(condition, 1.0, 0.0).astype(F32)


def chain(first, second, count, length, rate):
    s1, g1, sp1, gp1, a1, b1 = first
    s2, g2, sp2, gp2, a2, b2 = second
    step = jnp.exp(-float(length) * rate)
    whole = jnp.exp(-float(length * count) * rate)
    return (
        step * s1 + s2,
        g1 + whole * g2,
        step * (sp1 + float(length) * s1) + sp2,
        gp1 + whole * (gp2 + float(length * count) * g2),
        a1 + a2 + g2 * s1,
        b1 + b2 + gp2 * s1 + g2 * sp1,
    )


def kernel(
    dims,
    token_count,
    q_hbm,
    k_hbm,
    v_hbm,
    u_hbm,
    res_hbm,
    rate_hbm,
    w_ref,
    out_ref,
    gres_ref,
    glog_ref,
    qkvu_buf,
    small_buf,
    near_buf,
    far_buf,
    dz_buf,
    w_buf,
    in_sem,
    own_sem,
    near_send,
    near_recv,
    far_send,
    far_recv,
    near2_send,
    near2_recv,
    far2_send,
    far2_recv,
    dz_send,
    dz_recv,
    wz_send,
    wz_recv,
    wx_send,
    wx_recv,
    wc_send,
    wc_recv,
):
    nx, nzh, ny, nco, nzl = dims
    nb, na = ny * nco, nx * nzh
    ctx = lax.axis_index("ctx")
    zlo = lax.axis_index("ch")
    near = lax.rem(ctx, nb)
    far = ctx // nb
    core = lax.rem(ctx, nco)
    y = near // nco
    zh = lax.rem(far, nzh)
    x = far // nzh
    chans, span = qkvu_buf.shape[1:]
    modes = small_buf.shape[1]
    pairs = chans * modes
    blocks = pairs // LANES
    d_len = w_buf.shape[3]

    def ctx_of(px, pzh, py, pco):
        return ((px * nzh + pzh) * ny + py) * nco + pco

    def near_peer(away):
        return {"ctx": ctx_of(x, zh, lax.rem(y + away[0], ny), lax.rem(core + away[1], nco)), "ch": zlo}

    def line_peer(step):
        return {"ctx": ctx, "ch": lax.rem(zlo + step, nzl)}

    def x_peer(step):
        return {"ctx": ctx_of(lax.rem(x + step, nx), zh, y, core), "ch": zlo}

    def y_peer(step):
        return {"ctx": ctx_of(x, zh, lax.rem(y + step, ny), core), "ch": zlo}

    def cross_peer(step):
        return {"ctx": ctx_of(lax.rem(x + step, nx), 1 - zh, y, core), "ch": zlo}

    def by_distance(count):
        return sorted(range(count), key=lambda step: -min(step, count - step))

    near_ways = [(dy, dc) for dy in by_distance(ny) for dc in range(nco) if (dy, dc) != (0, 0)]
    x_ways = [step for step in by_distance(nx) if step]
    sibling = {"ctx": ctx_of(x, zh, y, lax.rem(core + 1, nco)), "ch": zlo}

    loads = [
        pltpu.make_async_copy(res_hbm, small_buf.at[0], in_sem.at[4]),
        pltpu.make_async_copy(rate_hbm, small_buf.at[1], in_sem.at[5]),
    ] + [
        pltpu.make_async_copy(ref, qkvu_buf.at[i], in_sem.at[i])
        for i, ref in enumerate((q_hbm, k_hbm, v_hbm, u_hbm))
    ]
    for load in loads:
        load.start()

    barrier = pltpu.get_barrier_semaphore()
    greeted = 0
    for peer_of, steps in ((line_peer, range(1, nzl)), (near_peer, near_ways), (x_peer, x_ways)):
        for step in steps:
            pl.semaphore_signal(barrier, inc=1, device_id=peer_of(step), device_id_type=MESH)
            greeted += 1

    @pl.when(zh == 0)
    def _():
        for step in range(nx):
            pl.semaphore_signal(barrier, inc=1, device_id=cross_peer(step), device_id_type=MESH)

    own_copy = pltpu.make_async_copy(
        w_ref.at[:, :, pl.ds(pl.multiple_of(zlo * d_len, LANES), d_len)], w_buf.at[0], own_sem
    )
    own_copy.start()

    row_chan = one_where(iota((pairs, chans), 0) // modes == iota((pairs, chans), 1))
    row_mode = one_where(lax.rem(iota((pairs, modes), 0), modes) == iota((pairs, modes), 1))
    lane_mode = one_where(iota((modes, pairs), 0) == lax.rem(iota((modes, pairs), 1), modes))
    lane_chan = one_where(iota((chans, pairs), 0) == iota((chans, pairs), 1) // modes)
    time = iota((pairs, span), 1).astype(F32)
    loads[0].wait()
    loads[1].wait()
    rates = small_buf[1]
    gain = jnp.sqrt(2.0 * rates)
    weight = small_buf[0] * gain
    rate_rows = dot(
        dot(row_chan, rates, ((1,), (1,))) * row_mode, jnp.ones((modes, LANES), F32)
    )
    spread = dot(jnp.concatenate([rates, weight], axis=1), lane_mode, ((0,), (0,)))
    rate_lane = jnp.sum(spread[:chans] * lane_chan, axis=0, keepdims=True)
    weight_diag = spread[chans:] * lane_chan

    def folded(row):
        return [row[:, LANES * i : LANES * (i + 1)] for i in range(blocks)]

    def fold(row):
        return jnp.concatenate(folded(row), axis=0)

    def unfold(rows):
        return jnp.concatenate([rows[i : i + 1] for i in range(blocks)], axis=1)

    def diagonal_rows(full):
        return fold(jnp.sum(full * lane_chan, axis=0, keepdims=True))

    rate4 = fold(rate_lane)
    falling = jnp.exp(-rate_rows * time)
    rising = jnp.exp(rate_rows * time)
    chunk_decay = jnp.exp(-float(span) * rate4)

    for load in loads[2:]:
        load.wait()
    key_f = qkvu_buf[1].astype(F32)
    value_f = qkvu_buf[2].astype(F32)
    up_f = qkvu_buf[3].astype(F32)
    mixed = key_f * value_f
    dgate = up_f * qkvu_buf[0].astype(F32)

    s4 = diagonal_rows(dot_nt(mixed, rising)) * chunk_decay
    g4 = diagonal_rows(dot_nt(dgate, falling))
    near_buf[near, 0 : 2 * blocks] = jnp.concatenate([s4, g4], axis=0)

    pl.semaphore_wait(barrier, jnp.where(zh == 0, greeted, greeted + nx))

    def make(src, dst, send, recv, peer):
        return pltpu.make_async_remote_copy(
            src_ref=src,
            dst_ref=dst,
            send_sem=send,
            recv_sem=recv,
            device_id=peer,
            device_id_type=MESH,
        )

    first, rest = pl.ds(0, 2 * blocks), pl.ds(2 * blocks, 4 * blocks)

    def near_exchange(part, send, recv):
        view = near_buf.at[near, part]
        return [
            make(view, view, send.at[i], recv.at[i], near_peer(way))
            for i, way in enumerate(near_ways)
        ]

    def far_exchange(part, send, recv):
        view = far_buf.at[far, part]
        same = [
            make(view, view, send.at[step - 1], recv.at[step - 1], x_peer(step))
            for step in x_ways
        ]
        cross = [
            make(view, view, send.at[nx - 1 + step], recv.at[nx - 1 + step], cross_peer(step))
            for step in by_distance(nx)
        ]
        return same, cross

    def start(copies):
        for copy in copies:
            copy.start()

    def arrive(copies):
        for copy in copies:
            copy.wait_recv()

    near_copies = near_exchange(first, near_send, near_recv)
    start(near_copies)

    def half_view(slot, half, column):
        return w_buf.at[
            slot,
            :,
            pl.ds(half * HALF, HALF),
            pl.ds(pl.multiple_of(column * LANES, LANES), LANES),
        ]

    x_column = x * nco + core
    y_column = y * nco + core
    wz_copies = []
    for step in range(1, nzl):
        for half, column in ((0, x_column), (1, y_column)):
            peer = line_peer(step)
            sem = 2 * (step - 1) + half
            source = w_ref.at[
                :,
                pl.ds(half * HALF, HALF),
                pl.ds(pl.multiple_of(peer["ch"] * d_len + column * LANES, LANES), LANES),
            ]
            wz_copies.append(
                make(source, half_view(step, half, column), wz_send.at[sem], wz_recv.at[sem], peer)
            )
    start(wz_copies)

    def over_modes(values):
        return jnp.broadcast_to(values[:, None, :], (chans, modes, span)).reshape(pairs, span)

    def lane_sums(rows):
        return fold(dot_nt(jnp.ones((8, span), F32), rows)[0:1])

    mixed_rows = over_modes(mixed)
    dgate_rows = over_modes(dgate)
    upper = one_where(iota((span, span), 0) <= iota((span, span), 1))
    lower = one_where(iota((span, span), 0) >= iota((span, span), 1))
    forward = falling * dot(rising * mixed_rows, upper)
    backward = rising * dot(falling * dgate_rows, lower)
    conv = dot(weight_diag, forward)
    dmixed = dot(weight_diag, backward)

    steps = iota((chans, span), 1).astype(F32)
    near_buf[near, 2 * blocks : 6 * blocks] = jnp.concatenate(
        [
            diagonal_rows(dot_nt(mixed * (float(span) - steps), rising)) * chunk_decay,
            diagonal_rows(dot_nt(dgate * steps, falling)),
            diagonal_rows(dot_nt(dgate, forward)),
            lane_sums((forward - mixed_rows) * backward),
        ],
        axis=0,
    )
    near2_copies = near_exchange(rest, near2_send, near2_recv)
    start(near2_copies)

    def scan(pieces, here, decay):
        run = jnp.zeros_like(decay)
        before = run
        for i, (s, _) in enumerate(pieces):
            before = jnp.where(here == i, run, before)
            run = decay * run + s
        back = jnp.zeros_like(decay)
        after = back
        for i, (_, g) in reversed(list(enumerate(pieces))):
            after = jnp.where(here == i, back, after)
            back = decay * back + g
        return before, after, run, back

    def states_of(buf, count):
        return [(buf[i, 0:blocks], buf[i, blocks : 2 * blocks]) for i in range(count)]

    arrive(near_copies)
    near_states = states_of(near_buf, nb)
    before_near, after_near, s_group, g_group = scan(near_states, near, chunk_decay)
    far_buf[far, 0 : 2 * blocks] = jnp.concatenate([s_group, g_group], axis=0)
    same_copies, cross_copies = far_exchange(first, far_send, far_recv)

    @pl.when(zh == 1)
    def _():
        start(cross_copies)

    start(same_copies)

    def pieces_of(buf, count):
        return [
            tuple(buf[i, j * blocks : (j + 1) * blocks] for j in range(6)) for i in range(count)
        ]

    def chained(pieces, length):
        total = pieces[0]
        for i in range(1, len(pieces)):
            total = chain(total, pieces[i], i, length, rate4)
        return total

    arrive(near2_copies)
    group = chained(pieces_of(near_buf, nb), span)
    far_buf[far, 2 * blocks : 6 * blocks] = jnp.concatenate(group[2:], axis=0)
    same2_copies, cross2_copies = far_exchange(rest, far2_send, far2_recv)

    @pl.when(zh == 1)
    def _():
        start(cross2_copies)

    start(same2_copies)

    arrive(wz_copies)

    def column_copy(half, column, send, recv, peer):
        view = w_buf.at[
            pl.ds(1, nzl - 1),
            :,
            pl.ds(half * HALF, HALF),
            pl.ds(pl.multiple_of(column * LANES, LANES), LANES),
        ]
        return make(view, view, send, recv, peer)

    wx_copies, wc_copies = [], []
    for half, count, peer_of, column in ((0, nx, x_peer, x_column), (1, ny, y_peer, y_column)):
        for step in range(1, count):
            sem = half * (nx - 1) + step - 1
            wx_copies.append(
                column_copy(half, column, wx_send.at[sem], wx_recv.at[sem], peer_of(step))
            )
    start(wx_copies)
    for half, column in ((0, x_column), (1, y_column)):
        wc_copies.append(column_copy(half, column, wc_send.at[half], wc_recv.at[half], sibling))
    start(wc_copies)

    arrive(same_copies)
    arrive(cross_copies)

    @pl.when(zh == 0)
    def _():
        start(cross_copies)
        start(cross2_copies)

    before_far, after_far, _, _ = scan(
        states_of(far_buf, na), far, jnp.exp(-float(span * nb) * rate4)
    )
    from_start = (near * span).astype(F32)
    to_end = ((nb - 1 - near) * span).astype(F32)
    before = before_near + jnp.exp(-rate4 * from_start) * before_far
    after = after_near + jnp.exp(-rate4 * to_end) * after_far

    conv = conv + dot(weight_diag * unfold(before), falling)
    dmixed = dmixed + dot(weight_diag * unfold(after * chunk_decay), rising)
    dz_buf[0, 0] = (up_f * conv).astype(jnp.bfloat16)
    dz_buf[0, 1] = (dmixed * value_f).astype(jnp.bfloat16)
    dz_buf[0, 2] = (dmixed * key_f).astype(jnp.bfloat16)
    dz_copies = [
        make(dz_buf.at[0], dz_buf.at[step], dz_send.at[step - 1], dz_recv.at[step - 1], line_peer(step))
        for step in range(1, nzl)
    ]
    start(dz_copies)

    index = 0
    for half, count, place, base in ((0, nx, x, 0), (1, ny, y, nx - 1)):
        for step in range(1, count):
            wx_copies[index].wait_recv()
            column = lax.rem(place - step + count, count) * nco + core
            sem = 2 + base + step - 1
            wc_copies.append(column_copy(half, column, wc_send.at[sem], wc_recv.at[sem], sibling))
            wc_copies[-1].start()
            index += 1

    arrive(same2_copies)
    arrive(cross2_copies)
    total = chained(pieces_of(far_buf, na), span * nb)
    sums = dot_nt(
        lane_mode,
        jnp.concatenate([lane_chan * unfold(total[4]), lane_chan * unfold(total[5])], axis=0),
    )
    same, apart = sums[:, :chans], sums[:, chans:]
    scale = 1.0 / math.sqrt(float(token_count))
    gres_ref[...] = same * gain * scale
    glog_ref[...] = weight * (0.5 * same - rates * apart) * scale

    own_copy.wait()
    arrive(wc_copies)
    arrive(dz_copies)
    rows = nzl * 3 * chans
    product = dot(
        dz_buf[...].reshape(rows, span), w_buf[...].reshape(rows, d_len), ((0,), (0,)), None
    )
    out_ref[...] = product.T.astype(jnp.bfloat16)

    for copies in (
        near_copies,
        near2_copies,
        same_copies,
        cross_copies,
        same2_copies,
        cross2_copies,
        wz_copies,
        wx_copies,
        wc_copies,
        dz_copies,
    ):
        for copy in copies:
            copy.wait_send()


def per_device(dims, queries, keys, values, upstream, residues, rates, w_in):
    nx, nzh, ny, nco, nzl = dims
    nb, na = ny * nco, nx * nzh
    chans, span = queries.shape
    modes = residues.shape[1]
    d_len = w_in.shape[2] // nzl
    states = (6 * chans * modes // LANES, LANES)
    vmem = pl.BlockSpec(memory_space=pltpu.VMEM)
    dma = pltpu.SemaphoreType.DMA
    outs = (
        jax.ShapeDtypeStruct((d_len, span), jnp.bfloat16),
        jax.ShapeDtypeStruct((modes, chans), F32),
        jax.ShapeDtypeStruct((modes, chans), F32),
    )
    grad_input, grad_residues, grad_lograte = pl.pallas_call(
        functools.partial(kernel, dims, span * na * nb),
        out_shape=outs,
        in_specs=[pl.BlockSpec(memory_space=pltpu.HBM)] * 7,
        out_specs=(vmem, vmem, vmem),
        scratch_shapes=[
            pltpu.VMEM((4, chans, span), jnp.bfloat16),
            pltpu.VMEM((2, modes, chans), F32),
            pltpu.VMEM((nb,) + states, F32),
            pltpu.VMEM((na,) + states, F32),
            pltpu.VMEM((nzl, 3, chans, span), jnp.bfloat16),
            pltpu.VMEM((nzl, 3, chans, d_len), jnp.bfloat16),
            dma((6,)),
            dma,
            dma((nb - 1,)),
            dma((nb - 1,)),
            dma((na - 1,)),
            dma((na - 1,)),
            dma((nb - 1,)),
            dma((nb - 1,)),
            dma((na - 1,)),
            dma((na - 1,)),
            dma((nzl - 1,)),
            dma((nzl - 1,)),
            dma((2 * (nzl - 1),)),
            dma((2 * (nzl - 1),)),
            dma((nx + ny - 2,)),
            dma((nx + ny - 2,)),
            dma((nx + ny,)),
            dma((nx + ny,)),
        ],
        compiler_params=pltpu.CompilerParams(
            collective_id=0, has_side_effects=True, vmem_limit_bytes=40 * 1024 * 1024
        ),
        cost_estimate=pl.CostEstimate(
            flops=2 * 3 * chans * nzl * d_len * span, bytes_accessed=2 * w_in.size, transcendentals=0
        ),
    )(*[pltpu.with_memory_space_constraint(a, pltpu.HBM) for a in (queries, keys, values, upstream, residues.T, rates.T, w_in)])
    return grad_input, grad_residues.T, grad_lograte.T


def solution(mesh, dims=(4, 2, 4, 2, 8)):
    return jax.shard_map(
        functools.partial(per_device, dims),
        mesh=mesh,
        in_specs=(
            P("ch", "ctx"),
            P("ch", "ctx"),
            P("ch", "ctx"),
            P("ch", "ctx"),
            P("ch", None),
            P("ch", None),
            P(None, "ch", None),
        ),
        out_specs=(P("ch", "ctx"), P("ch", None), P("ch", None)),
        check_vma=False,
    )
```

time: 55.9 us -> 47.6 us (0.85)
  the two profiles are of different devices: /device:TPU:64 before, /device:TPU:480 now
where the time goes in v2:
time: 47.6 us; the launch traced here: 47.5 us
  Pallas kernels  45 us (95%)
  local copies, waits for them, and re-layouts  1.9 us (4%)
  between operations  0.64 us (1%)
    pallas_call x1, Pallas kernels, per_device(): pl.pallas_call(functools.partial(kernel, dims, span * na * nb), out_shape...  45 us
    unnamed x3, local copies, waits for them, and re-layouts  1.9 us

profile of v2, /device:TPU:480, one launch (start us, length us, event | category | flops | bytes accessed | tf_op | source)
XLA Modules:
  0.0 47.5 jit_solution(11408585587327463188)
XLA Ops:
  0.6 45.0 %shard_map.94 = (bf16[1024,128]{1,0:T(8,128)(2,1)S(1)}, f32[16,32]{1,0:T(8,128)S(1)}, f32[16,32]{1,0:T(8,128)S(1)}) custom-call(bf16[32,128]{1,0:T(8,128)(2,1)} %q_hbm.1, bf16[32,128]{1,0:T(8,128)(2,1)} %k_hbm.1, bf16[32,128]{1,0:T(8,128)(2,1)} %v_hbm.1, bf16[32,128]{1,0:T(8,128)(2,1)} %u_hbm.1, f32[16,32]{1,0:T(8,128)} %bitcast.6, f32[16,32]{1,0:T(8,128)} %bitcast.7, ...), custom_call_target="tpu_custom_call" | custom-call | flops 201326592 | bytes 1572864 | tf_op jit(solution)/shard_map/pallas_call | solution.py:461
  45.6 0.7 %copy.13 = bf16[1024,128]{1,0:T(8,128)(2,1)} copy(bf16[1024,128]{1,0:T(8,128)(2,1)S(1)} %get-tuple-element.12) | data formatting | bytes 524288
  46.3 0.6 %copy.14 = f32[32,16]{0,1:T(8,128)} copy(f32[32,16]{0,1:T(8,128)S(1)} %bitcast.5) | data formatting | bytes 4096
  46.9 0.6 %copy.15 = f32[32,16]{0,1:T(8,128)} copy(f32[32,16]{0,1:T(8,128)S(1)} %bitcast.4) | data formatting | bytes 4096

commit v3 on v0

v3 whole, which is shorter than its diff:
```python
import functools
import math

import jax
import jax.numpy as jnp
from jax import lax
from jax.experimental import pallas as pl
from jax.experimental.pallas import tpu as pltpu
from jax.sharding import PartitionSpec as P

MESH = pl.DeviceIdType.MESH
HIGHEST = lax.Precision.HIGHEST
F32 = jnp.float32
LANES = 128
HALF = 16
CLOSE = 3


def dot(lhs, rhs, dims=((1,), (0,)), precision=HIGHEST):
    return lax.dot_general(
        lhs, rhs, (dims, ((), ())), precision=precision, preferred_element_type=F32
    )


def dot_nt(lhs, rhs):
    return dot(lhs, rhs, ((1,), (1,)))


def split(values):
    high = values.astype(jnp.bfloat16)
    return high, (values - high.astype(F32)).astype(jnp.bfloat16)


def dot_split(lhs, rhs, dims=((1,), (0,))):
    high, low = split(lhs)
    rows = lhs.shape[0]
    both = dot(jnp.concatenate([high, low], axis=0), rhs[0], dims, None)
    return both[:rows] + both[rows:] + dot(high, rhs[1], dims, None)


def iota(shape, dim):
    return lax.broadcasted_iota(jnp.int32, shape, dim)


def one_where(condition):
    return jnp.where(condition, 1.0, 0.0).astype(F32)


def chain(first, second, count, length, rate):
    s1, g1, sp1, gp1, a1, b1 = first
    s2, g2, sp2, gp2, a2, b2 = second
    step = jnp.exp(-float(length) * rate)
    whole = jnp.exp(-float(length * count) * rate)
    return (
        step * s1 + s2,
        g1 + whole * g2,
        step * (sp1 + float(length) * s1) + sp2,
        gp1 + whole * (gp2 + float(length * count) * g2),
        a1 + a2 + g2 * s1,
        b1 + b2 + gp2 * s1 + g2 * sp1,
    )


def kernel(dims, token_count, semaphores, *refs):
    nx, nzh, ny, nco, nzl = dims
    nb, na = ny * nco, nx * nzh
    q_hbm, k_hbm, v_hbm, u_hbm, res_hbm, rate_hbm, w_ref, out_ref, gres_ref, glog_ref = refs[:10]
    small_buf, raw_buf, half_buf, far_buf, state_buf, late_buf, dz_buf, w_buf = refs[10:18]
    sems = dict(zip(semaphores, refs[18:]))
    ctx = lax.axis_index("ctx")
    zlo = lax.axis_index("ch")
    near = lax.rem(ctx, nb)
    far = ctx // nb
    core = lax.rem(ctx, nco)
    y = near // nco
    zh = lax.rem(far, nzh)
    x = far // nzh
    chans, span = raw_buf.shape[2:]
    modes = small_buf.shape[1]
    pairs = chans * modes
    blocks = pairs // LANES
    d_len = w_buf.shape[3]

    def ctx_of(px, pzh, py, pco):
        return ((px * nzh + pzh) * ny + py) * nco + pco

    def plane_peer(away):
        dx, dy, dc = away
        there = ctx_of(lax.rem(x + dx, nx), zh, lax.rem(y + dy, ny), lax.rem(core + dc, nco))
        return {"ctx": there, "ch": zlo}

    def line_peer(step):
        return {"ctx": ctx, "ch": lax.rem(zlo + step, nzl)}

    def x_peer(step):
        return {"ctx": ctx_of(lax.rem(x + step, nx), zh, y, core), "ch": zlo}

    def y_peer(step):
        return {"ctx": ctx_of(x, zh, lax.rem(y + step, ny), core), "ch": zlo}

    def by_distance(count):
        return sorted(range(count), key=lambda step: -min(step, count - step))

    def hops(away):
        return min(away[0], nx - away[0]) + min(away[1], ny - away[1])

    plane_ways = sorted(
        [(i, j, k) for i in range(nx) for j in range(ny) for k in range(nco)][1:],
        key=lambda away: -hops(away),
    )
    x_ways = [step for step in by_distance(nx) if step]
    y_ways = [step for step in by_distance(ny) if step]
    line_ways = list(range(1, nzl))
    sibling = plane_peer((0, 0, 1))
    twin = {"ctx": ctx_of(x, 1 - zh, y, core), "ch": zlo}

    loads = [
        pltpu.make_async_copy(res_hbm, small_buf.at[0], sems["load"].at[4]),
        pltpu.make_async_copy(rate_hbm, small_buf.at[1], sems["load"].at[5]),
    ] + [
        pltpu.make_async_copy(ref, raw_buf.at[0, i], sems["load"].at[i])
        for i, ref in enumerate((q_hbm, k_hbm, v_hbm, u_hbm))
    ]
    for load in loads:
        load.start()

    barrier = pltpu.get_barrier_semaphore()

    def greet(semaphore, peer):
        pl.semaphore_signal(semaphore, inc=1, device_id=peer, device_id_type=MESH)

    def on_line(offset):
        return jnp.logical_and(zlo + offset >= 0, zlo + offset < nzl)

    def line_at(offset):
        return {"ctx": ctx, "ch": zlo + offset}

    def greet_line(semaphore, offsets, also=True):
        for offset in offsets:
            pl.when(jnp.logical_and(on_line(offset), also))(
                functools.partial(greet, semaphore, line_at(offset))
            )

    def count_line(offsets):
        return sum(on_line(offset).astype(jnp.int32) for offset in offsets)

    close = [sign * d for d in range(1, CLOSE + 1) for sign in (1, -1)]
    apart_ways = [sign * d for d in range(CLOSE + 1, nzl) for sign in (1, -1)]
    greet_line(barrier, close)
    greet_line(barrier, apart_ways, zh == 0)
    for way in plane_ways:
        greet(barrier, plane_peer(way))

    @pl.when(zh == 0)
    def _():
        greet(barrier, twin)

    greeted = len(plane_ways) + jnp.where(zh == 0, nzl - 1, 1 + count_line(close))

    def make(src, dst, name, index, peer):
        return pltpu.make_async_remote_copy(
            src_ref=src,
            dst_ref=dst,
            send_sem=sems[name + "_send"].at[index],
            recv_sem=sems[name + "_recv"].at[index],
            device_id=peer,
            device_id_type=MESH,
        )

    def same_place(view, name, peer_of, ways, base=0):
        return [make(view, view, name, base + i, peer_of(way)) for i, way in enumerate(ways)]

    def start(copies):
        for copy in copies:
            copy.start()

    def arrive(copies):
        for copy in copies:
            copy.wait_recv()

    def folded(row):
        return [row[:, LANES * i : LANES * (i + 1)] for i in range(blocks)]

    def fold(row):
        return jnp.concatenate(folded(row), axis=0)

    def unfold(rows):
        return jnp.concatenate([rows[i : i + 1] for i in range(blocks)], axis=1)

    lane_mode = one_where(iota((modes, pairs), 0) == lax.rem(iota((modes, pairs), 1), modes))
    lane_chan = one_where(iota((chans, pairs), 0) == iota((chans, pairs), 1) // modes)
    time = iota((pairs, span), 1).astype(F32)
    upper = one_where(iota((span, span), 0) <= iota((span, span), 1)).astype(jnp.bfloat16)
    lower = one_where(iota((span, span), 0) >= iota((span, span), 1)).astype(jnp.bfloat16)

    def lane_sum(full):
        return jnp.sum(full * lane_chan, axis=0, keepdims=True)

    def diagonal_rows(full):
        return fold(lane_sum(full))

    def over_modes(values):
        return jnp.broadcast_to(values[:, None, :], (chans, modes, span)).reshape(pairs, span)

    def powers(rate_lane):
        high = rate_lane.astype(jnp.bfloat16).astype(F32)
        middle = (rate_lane - high).astype(jnp.bfloat16).astype(F32)
        parts = [high, middle, rate_lane - high - middle, jnp.zeros((HALF - 3, pairs), F32)]
        column = jnp.concatenate(parts, axis=0).astype(jnp.bfloat16)
        ones = jnp.ones((HALF, span), jnp.bfloat16)
        exponent = dot(column, ones, ((0,), (0,)), None) * time
        return jnp.exp(-exponent), jnp.exp(exponent)

    def sums_along(values, ones):
        high, low = split(values)
        return dot(high, ones, precision=None) + dot(low, ones, precision=None)

    nt = ((1,), (1,))

    loads[0].wait()
    loads[1].wait()
    rates = small_buf[1]
    gain = jnp.sqrt(2.0 * rates)
    weight = small_buf[0] * gain
    spread = dot(jnp.concatenate([rates, weight], axis=1), lane_mode, ((0,), (0,)))
    rate_lane = lane_sum(spread[:chans])
    weight_lane = lane_sum(spread[chans:])
    rate4, weight4 = fold(rate_lane), fold(weight_lane)
    falling, rising = powers(rate_lane)
    chunk_decay = jnp.exp(-float(span) * rate4)

    for load in loads[2:]:
        load.wait()
    query_f, key_f, value_f, up_f = (raw_buf[0, i].astype(F32) for i in range(4))
    mixed = key_f * value_f
    dgate = up_f * query_f
    falling_parts, rising_parts = split(falling), split(rising)
    s4 = diagonal_rows(dot_split(mixed, rising_parts, nt)) * chunk_decay
    g4 = diagonal_rows(dot_split(dgate, falling_parts, nt))
    here = x * nb + near
    half_buf[here, 0 : 2 * blocks] = jnp.concatenate([s4, g4], axis=0)

    pl.semaphore_wait(barrier, greeted)

    first, rest = pl.ds(0, 2 * blocks), pl.ds(2 * blocks, 4 * blocks)
    plane_copies = same_place(half_buf.at[here, first], "plane", plane_peer, plane_ways)
    start(plane_copies)

    @pl.when(zh == 1)
    def _():
        greet_line(sems["first"], (CLOSE, -CLOSE))

    per_core = nzl // nco
    half = x // (nx // 2)
    column = lax.rem(x, nx // 2) * ny + y

    def part_rows(rows_half):
        return pl.ds(pl.multiple_of(rows_half * HALF, HALF), HALF)

    def columns(begin, count):
        return pl.ds(pl.multiple_of(begin * LANES, LANES), count * LANES)

    def source_part(owner):
        return w_ref.at[:, part_rows(half), columns(owner * (d_len // LANES) + column, 1)]

    def part_of(slot):
        return w_buf.at[slot, :, part_rows(half), columns(column, 1)]

    own_part = pltpu.make_async_copy(source_part(zlo), part_of(0), sems["own"].at[0])
    wz_copies = []
    for i in range(per_core):
        slot = core * per_core + i
        peer = line_peer(slot)
        wz_copies.append(make(source_part(peer["ch"]), part_of(slot), "wz", i, peer))
    part = pl.ds(1, 2)
    kv_copies = [
        make(raw_buf.at[0, part], raw_buf.at[k, part], "kv", k - 1, line_peer(k)) for k in line_ways
    ]

    @pl.when(core == 0)
    def _():
        own_part.start()

    def start_line():
        pl.when(core != 0)(wz_copies[0].start)
        start(wz_copies[1:])
        start(kv_copies)

    pl.when(zh == 0)(start_line)

    mixed_rows = over_modes(mixed)
    forward = falling * sums_along(rising * mixed_rows, upper)
    backward = rising * sums_along(falling * over_modes(dgate), lower)
    forward_parts = split(forward)
    weight_diag = lane_chan * weight_lane
    conv = dot_split(weight_diag, forward_parts)
    dmixed = dot_split(weight_diag, split(backward))
    steps = iota((chans, span), 1).astype(F32)
    apart = split((forward - mixed_rows) * backward)
    ones = jnp.ones((HALF, span), jnp.bfloat16)
    apart_lane = (dot(ones, apart[0], nt, None) + dot(ones, apart[1], nt, None))[0:1]
    half_buf[here, 2 * blocks : 6 * blocks] = jnp.concatenate(
        [
            diagonal_rows(dot_split(mixed * (float(span) - steps), rising_parts, nt)) * chunk_decay,
            diagonal_rows(dot_split(dgate * steps, falling_parts, nt)),
            diagonal_rows(dot_split(dgate, forward_parts, nt)),
            fold(apart_lane),
        ],
        axis=0,
    )
    plane2_copies = same_place(half_buf.at[here, rest], "plane2", plane_peer, plane_ways)
    start(plane2_copies)

    @pl.when(zh == 1)
    def _():
        pl.semaphore_wait(sems["first"], count_line((CLOSE, -CLOSE)))
        greet_line(sems["second"], (CLOSE + 1, -CLOSE - 1))

    rate8 = jnp.concatenate([rate4, rate4], axis=0)
    is_state = iota((2 * blocks, LANES), 0) < blocks

    def decay(length, if_state, if_other):
        away = jnp.where(is_state, if_state, if_other).astype(F32)
        power = jnp.exp(-float(length) * rate8 * jnp.maximum(away, 0.0))
        return jnp.where(away >= 0.0, power, 0.0)

    group_len = span * nb
    to_own, to_opp = [], []
    for px in range(nx):
        ahead = nzh * (x - px)
        to_own.append(decay(group_len, ahead - 1, -ahead - 1))
        to_opp.append(decay(group_len, ahead - 2 * zh, -ahead + 2 * zh - 2))
    inside = decay(span, near, nb - 1 - near)
    use = jnp.concatenate([weight4, weight4 * chunk_decay], axis=0)

    def group_states(px):
        run = jnp.zeros_like(rate4)
        back = run
        before = run
        after = run
        for i in range(nb):
            before = jnp.where(near == i, run, before)
            run = chunk_decay * run + half_buf[px * nb + i, 0:blocks]
            j = nb - 1 - i
            after = jnp.where(near == j, back, after)
            back = chunk_decay * back + half_buf[px * nb + j, blocks : 2 * blocks]
        return jnp.concatenate([before, after], axis=0), jnp.concatenate([run, back], axis=0)

    arrive(plane_copies)
    own_states = jnp.zeros_like(rate8)
    opp_states = jnp.zeros_like(rate8)
    from_near = jnp.zeros_like(rate8)
    for px in range(nx):
        around, states = group_states(px)
        from_near = jnp.where(x == px, around, from_near)
        own_states = own_states + to_own[px] * states
        opp_states = opp_states + to_opp[px] * states
    state_buf[zh] = inside * opp_states
    twin_copies = [make(state_buf.at[zh], state_buf.at[zh], "twin", 0, twin)]

    @pl.when(zh == 1)
    def _():
        start(twin_copies)
        pl.semaphore_wait(sems["second"], count_line((CLOSE + 1, -CLOSE - 1)))
        start_line()

    def chained(pieces, length):
        total = pieces[0]
        for i in range(1, len(pieces)):
            total = chain(total, pieces[i], i, length, rate4)
        return total

    def piece(rows):
        return tuple(rows[j * blocks : (j + 1) * blocks] for j in range(6))

    arrive(plane2_copies)
    for px in range(nx):
        group = chained([piece(half_buf[px * nb + i]) for i in range(nb)], span)
        far_buf[zh, px] = jnp.concatenate(group, axis=0)
    twin2_copies = [make(far_buf.at[zh], far_buf.at[zh], "twin", 1, twin)]

    @pl.when(zh == 1)
    def _():
        start(twin2_copies)

    two = per_core // 2
    begin = core * per_core

    def across(slots, rows, cols):
        return w_buf.at[pl.ds(slots, two), :, rows, cols]

    x_peers = [(way, 0, 0) for way in x_ways]
    y_peers = [(0, way, 0) for way in y_ways]
    my_part = (part_rows(half), columns(column, 1))
    w2_copies = same_place(across(begin, *my_part), "w2", plane_peer, x_peers)
    w2_copies += same_place(across(begin + two, *my_part), "w2", plane_peer, y_peers, nx - 1)
    w3_copies = []
    for i in range(nx // 2):
        view = across(begin, pl.ds(0, 2 * HALF), columns(i * ny + y, 1))
        w3_copies += same_place(view, "w3", plane_peer, y_peers, i * (ny - 1))
    view = across(begin + two, part_rows(half), columns(lax.rem(x, nx // 2) * ny, ny))
    w3_copies += same_place(view, "w3", plane_peer, x_peers, nx // 2 * (ny - 1))
    whole = w_buf.at[pl.ds(begin, per_core)]
    w4_copies = [make(whole, whole, "w4", 0, sibling)]

    @pl.when(core == 0)
    def _():
        own_part.wait()

    @pl.when(core != 0)
    def _():
        wz_copies[0].wait_recv()

    arrive(wz_copies[1:])
    start(w2_copies)

    arrive(twin_copies)

    @pl.when(zh == 0)
    def _():
        start(twin_copies)
        start(twin2_copies)

    states = use * (from_near + inside * own_states + state_buf[1 - zh])
    conv = conv + dot_split(lane_chan * unfold(states[:blocks]), falling_parts)
    dmixed = dmixed + dot_split(lane_chan * unfold(states[blocks:]), rising_parts)
    late_buf[0, 0] = (up_f * conv).astype(jnp.bfloat16)
    late_buf[0, 1] = dmixed.astype(jnp.bfloat16)
    late_copies = [make(late_buf.at[0], late_buf.at[k], "late", k - 1, line_peer(k)) for k in line_ways]
    start(late_copies)
    dz_buf[0, 0] = late_buf[0, 0]
    dz_buf[0, 1] = (dmixed * value_f).astype(jnp.bfloat16)
    dz_buf[0, 2] = (dmixed * key_f).astype(jnp.bfloat16)

    arrive(w2_copies)
    start(w3_copies)
    arrive(w3_copies)
    start(w4_copies)

    arrive(kv_copies)
    arrive(w4_copies)
    arrive(late_copies)
    for k in line_ways:
        dmixed_k = late_buf[k, 1].astype(F32)
        dz_buf[k, 0] = late_buf[k, 0]
        dz_buf[k, 1] = (dmixed_k * raw_buf[k, 2].astype(F32)).astype(jnp.bfloat16)
        dz_buf[k, 2] = (dmixed_k * raw_buf[k, 1].astype(F32)).astype(jnp.bfloat16)
    rows = nzl * 3 * chans
    product = dot(
        dz_buf[...].reshape(rows, span), w_buf[...].reshape(rows, d_len), ((0,), (0,)), None
    )
    out_ref[...] = product.T.astype(jnp.bfloat16)

    arrive(twin2_copies)
    pieces = [piece(far_buf[h, px]) for px in range(nx) for h in range(nzh)]
    total = chained(pieces, group_len)
    sums = dot_nt(
        lane_mode,
        jnp.concatenate([lane_chan * unfold(total[4]), lane_chan * unfold(total[5])], axis=0),
    )
    same, apart = sums[:, :chans], sums[:, chans:]
    scale = 1.0 / math.sqrt(float(token_count))
    gres_ref[...] = same * gain * scale
    glog_ref[...] = weight * (0.5 * same - rates * apart) * scale

    @pl.when(core != 0)
    def _():
        wz_copies[0].wait_send()

    for copies in (
        plane_copies,
        plane2_copies,
        twin_copies,
        twin2_copies,
        wz_copies[1:],
        kv_copies,
        late_copies,
        w2_copies,
        w3_copies,
        w4_copies,
    ):
        for copy in copies:
            copy.wait_send()


def per_device(dims, queries, keys, values, upstream, residues, rates, w_in):
    nx, nzh, ny, nco, nzl = dims
    nb, na = ny * nco, nx * nzh
    chans, span = queries.shape
    modes = residues.shape[1]
    d_len = w_in.shape[2] // nzl
    pairs = chans * modes
    blocks = pairs // LANES
    vmem = pl.BlockSpec(memory_space=pltpu.VMEM)
    counts = {
        "plane": nx * nb - 1,
        "plane2": nx * nb - 1,
        "twin": 2,
        "wz": nzl // nco,
        "kv": nzl - 1,
        "late": nzl - 1,
        "w2": nx + ny - 2,
        "w3": nx // 2 * (ny - 1) + nx - 1,
        "w4": 1,
    }
    semaphores = {"load": 6, "own": 1}
    for name, count in counts.items():
        semaphores[name + "_send"] = count
        semaphores[name + "_recv"] = count
    arrays = [
        pltpu.with_memory_space_constraint(array, pltpu.HBM)
        for array in (queries, keys, values, upstream, residues.T, rates.T, w_in)
    ]
    grad_input, grad_residues, grad_lograte = pl.pallas_call(
        functools.partial(kernel, dims, span * na * nb, (*semaphores, "first", "second")),
        out_shape=(
            jax.ShapeDtypeStruct((d_len, span), jnp.bfloat16),
            jax.ShapeDtypeStruct((modes, chans), F32),
            jax.ShapeDtypeStruct((modes, chans), F32),
        ),
        in_specs=[pl.BlockSpec(memory_space=pltpu.HBM)] * 7,
        out_specs=(vmem, vmem, vmem),
        scratch_shapes=[
            pltpu.VMEM((2, modes, chans), F32),
            pltpu.VMEM((nzl, 4, chans, span), jnp.bfloat16),
            pltpu.VMEM((nx * nb, 6 * blocks, LANES), F32),
            pltpu.VMEM((nzh, nx, 6 * blocks, LANES), F32),
            pltpu.VMEM((nzh, 2 * blocks, LANES), F32),
            pltpu.VMEM((nzl, 2, chans, span), jnp.bfloat16),
            pltpu.VMEM((nzl, 3, chans, span), jnp.bfloat16),
            pltpu.VMEM((nzl, 3, chans, d_len), jnp.bfloat16),
        ]
        + [pltpu.SemaphoreType.DMA((count,)) for count in semaphores.values()]
        + [pltpu.SemaphoreType.REGULAR] * 2,
        compiler_params=pltpu.CompilerParams(
            collective_id=0, has_side_effects=True, vmem_limit_bytes=40 * 1024 * 1024
        ),
        cost_estimate=pl.CostEstimate(
            flops=2 * 3 * chans * nzl * d_len * span, bytes_accessed=2 * w_in.size, transcendentals=0
        ),
    )(*arrays)
    return grad_input, grad_residues.T, grad_lograte.T


def solution(mesh, dims=(4, 2, 4, 2, 8)):
    return jax.shard_map(
        functools.partial(per_device, dims),
        mesh=mesh,
        in_specs=(
            P("ch", "ctx"),
            P("ch", "ctx"),
            P("ch", "ctx"),
            P("ch", "ctx"),
            P("ch", None),
            P("ch", None),
            P(None, "ch", None),
        ),
        out_specs=(P("ch", "ctx"), P("ch", None), P("ch", None)),
        check_vma=False,
    )
```

time: 790 us -> 42.9 us (0.05)
  the two profiles are of different devices: /device:TPU:32 before, /device:TPU:2 now
where the time goes in v3:
time: 42.9 us; the launch traced here: 42.8 us
  Pallas kernels  40.2 us (94%)
  local copies, waits for them, and re-layouts  1.9 us (4%)
  between operations  0.64 us (1%)
    pallas_call x1, Pallas kernels, per_device(): pl.pallas_call(functools.partial(kernel, dims, span * na * nb, (*semaphor...  40.2 us
    unnamed x3, local copies, waits for them, and re-layouts  1.9 us

profile of v3, /device:TPU:2, one launch (start us, length us, event | category | flops | bytes accessed | tf_op | source)
XLA Modules:
  0.0 42.8 jit_solution(5765396323529864609)
XLA Ops:
  0.6 40.2 %shard_map.94 = (bf16[1024,128]{1,0:T(8,128)(2,1)S(1)}, f32[16,32]{1,0:T(8,128)S(1)}, f32[16,32]{1,0:T(8,128)S(1)}) custom-call(bf16[32,128]{1,0:T(8,128)(2,1)} %refs_0_.1, bf16[32,128]{1,0:T(8,128)(2,1)} %refs_1_.1, bf16[32,128]{1,0:T(8,128)(2,1)} %refs_2_.1, bf16[32,128]{1,0:T(8,128)(2,1)} %refs_3_.1, f32[16,32]{1,0:T(8,128)} %bitcast.6, ...), custom_call_target="tpu_custom_call" | custom-call | flops 201326592 | bytes 1572864 | tf_op jit(solution)/shard_map/pallas_call | solution.py:514
  40.9 0.7 %copy.13 = bf16[1024,128]{1,0:T(8,128)(2,1)} copy(bf16[1024,128]{1,0:T(8,128)(2,1)S(1)} %get-tuple-element.12) | data formatting | bytes 524288
  41.6 0.6 %copy.14 = f32[32,16]{0,1:T(8,128)} copy(f32[32,16]{0,1:T(8,128)S(1)} %bitcast.5) | data formatting | bytes 4096
  42.2 0.6 %copy.15 = f32[32,16]{0,1:T(8,128)} copy(f32[32,16]{0,1:T(8,128)S(1)} %bitcast.4) | data formatting | bytes 4096

commit v4 on v3

--- a/solution.py
+++ b/solution.py
@@ -65,8 +65,8 @@
     nx, nzh, ny, nco, nzl = dims
     nb, na = ny * nco, nx * nzh
     q_hbm, k_hbm, v_hbm, u_hbm, res_hbm, rate_hbm, w_ref, out_ref, gres_ref, glog_ref = refs[:10]
-    small_buf, raw_buf, half_buf, far_buf, state_buf, late_buf, dz_buf, w_buf = refs[10:18]
-    sems = dict(zip(semaphores, refs[18:]))
+    small_buf, raw_buf, half_buf, state_buf, tuple_buf, total_buf, late_buf, dz_buf, w_buf = refs[10:19]
+    sems = dict(zip(semaphores, refs[19:]))
     ctx = lax.axis_index("ctx")
     zlo = lax.axis_index("ch")
     near = lax.rem(ctx, nb)
@@ -112,7 +112,14 @@
     y_ways = [step for step in by_distance(ny) if step]
     line_ways = list(range(1, nzl))
     sibling = plane_peer((0, 0, 1))
+    near_ways = [way for way in plane_ways if way[0] == 0]
     twin = {"ctx": ctx_of(x, 1 - zh, y, core), "ch": zlo}
+
+    def member(group):
+        return {"ctx": group * nb + near, "ch": zlo}
+
+    collects = near == far
+    far_target = lax.rem(near, nzh)
 
     loads = [
         pltpu.make_async_copy(res_hbm, small_buf.at[0], sems["load"].at[4]),
@@ -155,7 +162,15 @@
     def _():
         greet(barrier, twin)
 
-    greeted = len(plane_ways) + jnp.where(zh == 0, nzl - 1, 1 + count_line(close))
+        @pl.when(collects)
+        def _():
+            for px in range(nx):
+                greet(barrier, member(px * nzh + 1))
+
+        pl.when(far_target == 1)(functools.partial(greet, barrier, member(near)))
+
+    from_first = 1 + jnp.where(far_target == 0, 1, 0) + jnp.where(collects, nx, 0)
+    greeted = len(plane_ways) + jnp.where(zh == 0, nzl - 1, from_first + count_line(close))
 
     def make(src, dst, name, index, peer):
         return pltpu.make_async_remote_copy(
@@ -238,17 +253,23 @@
     s4 = diagonal_rows(dot_split(mixed, rising_parts, nt)) * chunk_decay
     g4 = diagonal_rows(dot_split(dgate, falling_parts, nt))
     here = x * nb + near
+    first, rest = pl.ds(0, 2 * blocks), pl.ds(2 * blocks, 4 * blocks)
     half_buf[here, 0 : 2 * blocks] = jnp.concatenate([s4, g4], axis=0)
 
     pl.semaphore_wait(barrier, greeted)
 
-    first, rest = pl.ds(0, 2 * blocks), pl.ds(2 * blocks, 4 * blocks)
     plane_copies = same_place(half_buf.at[here, first], "plane", plane_peer, plane_ways)
+
     start(plane_copies)
 
     @pl.when(zh == 1)
     def _():
         greet_line(sems["first"], (CLOSE, -CLOSE))
+
+        @pl.when(collects)
+        def _():
+            for px in range(nx):
+                greet(sems["third"], member(px * nzh))
 
     per_core = nzl // nco
     half = x // (nx // 2)
@@ -308,8 +329,8 @@
         ],
         axis=0,
     )
-    plane2_copies = same_place(half_buf.at[here, rest], "plane2", plane_peer, plane_ways)
-    start(plane2_copies)
+    near_copies = same_place(half_buf.at[here, rest], "near", plane_peer, near_ways)
+    start(near_copies)
 
     @pl.when(zh == 1)
     def _():
@@ -347,15 +368,15 @@
         return jnp.concatenate([before, after], axis=0), jnp.concatenate([run, back], axis=0)
 
     arrive(plane_copies)
-    own_states = jnp.zeros_like(rate8)
-    opp_states = jnp.zeros_like(rate8)
+    far_states = jnp.zeros_like(rate8)
+    twin_states = jnp.zeros_like(rate8)
     from_near = jnp.zeros_like(rate8)
     for px in range(nx):
         around, states = group_states(px)
         from_near = jnp.where(x == px, around, from_near)
-        own_states = own_states + to_own[px] * states
-        opp_states = opp_states + to_opp[px] * states
-    state_buf[zh] = inside * opp_states
+        far_states = far_states + to_own[px] * states
+        twin_states = twin_states + to_opp[px] * states
+    state_buf[zh] = twin_states
     twin_copies = [make(state_buf.at[zh], state_buf.at[zh], "twin", 0, twin)]
 
     @pl.when(zh == 1)
@@ -373,15 +394,13 @@
     def piece(rows):
         return tuple(rows[j * blocks : (j + 1) * blocks] for j in range(6))
 
-    arrive(plane2_copies)
-    for px in range(nx):
-        group = chained([piece(half_buf[px * nb + i]) for i in range(nb)], span)
-        far_buf[zh, px] = jnp.concatenate(group, axis=0)
-    twin2_copies = [make(far_buf.at[zh], far_buf.at[zh], "twin", 1, twin)]
-
-    @pl.when(zh == 1)
-    def _():
-        start(twin2_copies)
+    arrive(near_copies)
+    pieces = [piece(half_buf[x * nb + i]) for i in range(nb)]
+    tuple_buf[far] = jnp.concatenate(chained(pieces, span), axis=0)
+    tuple_copy = make(tuple_buf.at[far], tuple_buf.at[far], "tuple", far, member(near))
+    hands_on = jnp.logical_not(collects)
+    waits = jnp.logical_and(zh == 0, far_target == 1)
+    pl.when(jnp.logical_and(hands_on, jnp.logical_not(waits)))(tuple_copy.start)
 
     two = per_core // 2
     begin = core * per_core
@@ -403,25 +422,19 @@
     whole = w_buf.at[pl.ds(begin, per_core)]
     w4_copies = [make(whole, whole, "w4", 0, sibling)]
 
-    @pl.when(core == 0)
-    def _():
-        own_part.wait()
-
-    @pl.when(core != 0)
-    def _():
-        wz_copies[0].wait_recv()
-
+    pl.when(core == 0)(own_part.wait)
+    pl.when(core != 0)(wz_copies[0].wait_recv)
     arrive(wz_copies[1:])
     start(w2_copies)
-
+    arrive(w2_copies)
+    start(w3_copies)
     arrive(twin_copies)
 
     @pl.when(zh == 0)
     def _():
         start(twin_copies)
-        start(twin2_copies)
-
-    states = use * (from_near + inside * own_states + state_buf[1 - zh])
+
+    states = use * (from_near + inside * (far_states + state_buf[1 - zh]))
     conv = conv + dot_split(lane_chan * unfold(states[:blocks]), falling_parts)
     dmixed = dmixed + dot_split(lane_chan * unfold(states[blocks:]), rising_parts)
     late_buf[0, 0] = (up_f * conv).astype(jnp.bfloat16)
@@ -432,10 +445,34 @@
     dz_buf[0, 1] = (dmixed * value_f).astype(jnp.bfloat16)
     dz_buf[0, 2] = (dmixed * key_f).astype(jnp.bfloat16)
 
-    arrive(w2_copies)
-    start(w3_copies)
+    @pl.when(waits)
+    def _():
+        pl.semaphore_wait(sems["third"], 1)
+        tuple_copy.start()
+
     arrive(w3_copies)
     start(w4_copies)
+
+    def hand_out(way, index):
+        return pltpu.make_async_remote_copy(
+            src_ref=total_buf,
+            dst_ref=total_buf,
+            send_sem=sems["total_send"].at[index],
+            recv_sem=sems["total_recv"].at[0],
+            device_id=plane_peer(way),
+            device_id_type=MESH,
+        )
+
+    total_copies = [hand_out(way, i) for i, way in enumerate(near_ways)]
+
+    @pl.when(collects)
+    def _():
+        for a in range(na):
+            arrived = make(tuple_buf.at[a], tuple_buf.at[a], "tuple", a, twin)
+            pl.when(far != a)(arrived.wait_recv)
+        whole_run = chained([piece(tuple_buf[a]) for a in range(na)], group_len)
+        total_buf[...] = jnp.concatenate(whole_run[4:], axis=0)
+        start(total_copies)
 
     arrive(kv_copies)
     arrive(w4_copies)
@@ -451,27 +488,29 @@
     )
     out_ref[...] = product.T.astype(jnp.bfloat16)
 
-    arrive(twin2_copies)
-    pieces = [piece(far_buf[h, px]) for px in range(nx) for h in range(nzh)]
-    total = chained(pieces, group_len)
+    pl.when(hands_on)(total_copies[0].wait_recv)
+    total = total_buf[...]
     sums = dot_nt(
         lane_mode,
-        jnp.concatenate([lane_chan * unfold(total[4]), lane_chan * unfold(total[5])], axis=0),
+        jnp.concatenate([lane_chan * unfold(total[:blocks]), lane_chan * unfold(total[blocks:])], axis=0),
     )
     same, apart = sums[:, :chans], sums[:, chans:]
     scale = 1.0 / math.sqrt(float(token_count))
     gres_ref[...] = same * gain * scale
     glog_ref[...] = weight * (0.5 * same - rates * apart) * scale
 
-    @pl.when(core != 0)
-    def _():
-        wz_copies[0].wait_send()
+    pl.when(core != 0)(wz_copies[0].wait_send)
+    pl.when(hands_on)(tuple_copy.wait_send)
+
+    @pl.when(collects)
+    def _():
+        for copy in total_copies:
+            copy.wait_send()
 
     for copies in (
         plane_copies,
-        plane2_copies,
+        near_copies,
         twin_copies,
-        twin2_copies,
         wz_copies[1:],
         kv_copies,
         late_copies,
@@ -481,6 +520,12 @@
     ):
         for copy in copies:
             copy.wait_send()
+
+
+def finish(out_in, gres_in, glog_in, out_ref, gres_ref, glog_ref):
+    out_ref[...] = out_in[...]
+    gres_ref[...] = gres_in[...]
+    glog_ref[...] = glog_in[...]
 
 
 def per_device(dims, queries, keys, values, upstream, residues, rates, w_in):
@@ -494,8 +539,10 @@
     vmem = pl.BlockSpec(memory_space=pltpu.VMEM)
     counts = {
         "plane": nx * nb - 1,
-        "plane2": nx * nb - 1,
-        "twin": 2,
+        "near": nb - 1,
+        "tuple": na,
+        "total": nb - 1,
+        "twin": 1,
         "wz": nzl // nco,
         "kv": nzl - 1,
         "late": nzl - 1,
@@ -511,8 +558,8 @@
         pltpu.with_memory_space_constraint(array, pltpu.HBM)
         for array in (queries, keys, values, upstream, residues.T, rates.T, w_in)
     ]
-    grad_input, grad_residues, grad_lograte = pl.pallas_call(
-        functools.partial(kernel, dims, span * na * nb, (*semaphores, "first", "second")),
+    results = pl.pallas_call(
+        functools.partial(kernel, dims, span * na * nb, (*semaphores, "first", "second", "third")),
         out_shape=(
             jax.ShapeDtypeStruct((d_len, span), jnp.bfloat16),
             jax.ShapeDtypeStruct((modes, chans), F32),
@@ -524,14 +571,15 @@
             pltpu.VMEM((2, modes, chans), F32),
             pltpu.VMEM((nzl, 4, chans, span), jnp.bfloat16),
             pltpu.VMEM((nx * nb, 6 * blocks, LANES), F32),
-            pltpu.VMEM((nzh, nx, 6 * blocks, LANES), F32),
             pltpu.VMEM((nzh, 2 * blocks, LANES), F32),
+            pltpu.VMEM((na, 6 * blocks, LANES), F32),
+            pltpu.VMEM((2 * blocks, LANES), F32),
             pltpu.VMEM((nzl, 2, chans, span), jnp.bfloat16),
             pltpu.VMEM((nzl, 3, chans, span), jnp.bfloat16),
             pltpu.VMEM((nzl, 3, chans, d_len), jnp.bfloat16),
         ]
         + [pltpu.SemaphoreType.DMA((count,)) for count in semaphores.values()]
-        + [pltpu.SemaphoreType.REGULAR] * 2,
+        + [pltpu.SemaphoreType.REGULAR] * 3,
         compiler_params=pltpu.CompilerParams(
             collective_id=0, has_side_effects=True, vmem_limit_bytes=40 * 1024 * 1024
         ),
@@ -539,6 +587,17 @@
             flops=2 * 3 * chans * nzl * d_len * span, bytes_accessed=2 * w_in.size, transcendentals=0
         ),
     )(*arrays)
+    grad_input, grad_residues, grad_lograte = pl.pallas_call(
+        finish,
+        out_shape=(
+            jax.ShapeDtypeStruct((d_len, span), jnp.bfloat16),
+            jax.ShapeDtypeStruct((modes, chans), F32),
+            jax.ShapeDtypeStruct((modes, chans), F32),
+        ),
+        in_specs=[vmem] * 3,
+        out_specs=(vmem,) * 3,
+        compiler_params=pltpu.CompilerParams(vmem_limit_bytes=4 * 1024 * 1024),
+    )(*results)
     return grad_input, grad_residues.T, grad_lograte.T
 
 

time: 42.9 us -> 39.3 us (0.916)
  the two profiles are of different devices: /device:TPU:2 before, /device:TPU:73 now
where the time goes in v4:
time: 39.3 us; the launch traced here: 39.1 us
  Pallas kernels  38.5 us (98%)
  between operations  0.64 us (2%)
    pallas_call x1, Pallas kernels, per_device(): pl.pallas_call(functools.partial(kernel, dims, span * na * nb, (*semaphor...  37.7 us

profile of v4, /device:TPU:73, one launch (start us, length us, event | category | flops | bytes accessed | tf_op | source)
XLA Modules:
  0.0 39.1 jit_solution(13395954665790862736)
XLA Ops:
  0.6 37.7 %shard_map.94 = (bf16[1024,128]{1,0:T(8,128)(2,1)S(1)}, f32[16,32]{1,0:T(8,128)S(1)}, f32[16,32]{1,0:T(8,128)S(1)}) custom-call(bf16[32,128]{1,0:T(8,128)(2,1)} %refs_0_.1, bf16[32,128]{1,0:T(8,128)(2,1)} %refs_1_.1, bf16[32,128]{1,0:T(8,128)(2,1)} %refs_2_.1, bf16[32,128]{1,0:T(8,128)(2,1)} %refs_3_.1, f32[16,32]{1,0:T(8,128)} %bitcast.4, ...), custom_call_target="tpu_custom_call" | custom-call | flops 201326592 | bytes 1572864 | tf_op jit(solution)/shard_map/pallas_call | solution.py:561
  38.4 0.7 %shard_map.95 = (bf16[1024,128]{1,0:T(8,128)(2,1)}, f32[16,32]{1,0:T(8,128)}, f32[16,32]{1,0:T(8,128)}) custom-call(bf16[1024,128]{1,0:T(8,128)(2,1)S(1)} %get-tuple-element.9.out_in, f32[16,32]{1,0:T(8,128)S(1)} %get-tuple-element.10.gres_in, f32[16,32]{1,0:T(8,128)S(1)} %get-tuple-element.11.glog_in), custom_call_target="tpu_custom_call" | custom-call | tf_op jit(solution)/shard_map/pallas_call | solution.py:590

commit v5 on v4

--- a/solution.py
+++ b/solution.py
@@ -119,7 +119,8 @@
         return {"ctx": group * nb + near, "ch": zlo}
 
     collects = near == far
-    far_target = lax.rem(near, nzh)
+    same_half = lax.rem(near, nzh) == zh
+    opp_far = x * nzh + 1 - zh
 
     loads = [
         pltpu.make_async_copy(res_hbm, small_buf.at[0], sems["load"].at[4]),
@@ -153,24 +154,13 @@
 
     close = [sign * d for d in range(1, CLOSE + 1) for sign in (1, -1)]
     apart_ways = [sign * d for d in range(CLOSE + 1, nzl) for sign in (1, -1)]
+    pl.when(zh == 0)(functools.partial(greet, barrier, twin))
     greet_line(barrier, close)
     greet_line(barrier, apart_ways, zh == 0)
     for way in plane_ways:
         greet(barrier, plane_peer(way))
 
-    @pl.when(zh == 0)
-    def _():
-        greet(barrier, twin)
-
-        @pl.when(collects)
-        def _():
-            for px in range(nx):
-                greet(barrier, member(px * nzh + 1))
-
-        pl.when(far_target == 1)(functools.partial(greet, barrier, member(near)))
-
-    from_first = 1 + jnp.where(far_target == 0, 1, 0) + jnp.where(collects, nx, 0)
-    greeted = len(plane_ways) + jnp.where(zh == 0, nzl - 1, from_first + count_line(close))
+    greeted = len(plane_ways) + jnp.where(zh == 0, nzl - 1, 1 + count_line(close))
 
     def make(src, dst, name, index, peer):
         return pltpu.make_async_remote_copy(
@@ -266,11 +256,6 @@
     def _():
         greet_line(sems["first"], (CLOSE, -CLOSE))
 
-        @pl.when(collects)
-        def _():
-            for px in range(nx):
-                greet(sems["third"], member(px * nzh))
-
     per_core = nzl // nco
     half = x // (nx // 2)
     column = lax.rem(x, nx // 2) * ny + y
@@ -305,7 +290,6 @@
     def start_line():
         pl.when(core != 0)(wz_copies[0].start)
         start(wz_copies[1:])
-        start(kv_copies)
 
     pl.when(zh == 0)(start_line)
 
@@ -397,10 +381,13 @@
     arrive(near_copies)
     pieces = [piece(half_buf[x * nb + i]) for i in range(nb)]
     tuple_buf[far] = jnp.concatenate(chained(pieces, span), axis=0)
-    tuple_copy = make(tuple_buf.at[far], tuple_buf.at[far], "tuple", far, member(near))
+    target = {"ctx": jnp.where(same_half, member(near)["ctx"], twin["ctx"]), "ch": zlo}
+    tuple_copy = make(tuple_buf.at[far], tuple_buf.at[far], "tuple", far, target)
+    pass_copy = make(tuple_buf.at[opp_far], tuple_buf.at[opp_far], "tuple", opp_far, member(near))
     hands_on = jnp.logical_not(collects)
-    waits = jnp.logical_and(zh == 0, far_target == 1)
-    pl.when(jnp.logical_and(hands_on, jnp.logical_not(waits)))(tuple_copy.start)
+    passes = jnp.logical_and(same_half, hands_on)
+    crosses = jnp.logical_not(same_half)
+    pl.when(jnp.logical_or(passes, jnp.logical_and(crosses, zh == 1)))(tuple_copy.start)
 
     two = per_core // 2
     begin = core * per_core
@@ -426,6 +413,7 @@
     pl.when(core != 0)(wz_copies[0].wait_recv)
     arrive(wz_copies[1:])
     start(w2_copies)
+    start(kv_copies)
     arrive(w2_copies)
     start(w3_copies)
     arrive(twin_copies)
@@ -445,10 +433,12 @@
     dz_buf[0, 1] = (dmixed * value_f).astype(jnp.bfloat16)
     dz_buf[0, 2] = (dmixed * key_f).astype(jnp.bfloat16)
 
-    @pl.when(waits)
-    def _():
-        pl.semaphore_wait(sems["third"], 1)
-        tuple_copy.start()
+    pl.when(jnp.logical_and(crosses, zh == 0))(tuple_copy.start)
+
+    @pl.when(passes)
+    def _():
+        pass_copy.wait_recv()
+        pass_copy.start()
 
     arrive(w3_copies)
     start(w4_copies)
@@ -501,6 +491,7 @@
 
     pl.when(core != 0)(wz_copies[0].wait_send)
     pl.when(hands_on)(tuple_copy.wait_send)
+    pl.when(passes)(pass_copy.wait_send)
 
     @pl.when(collects)
     def _():
@@ -559,7 +550,7 @@
         for array in (queries, keys, values, upstream, residues.T, rates.T, w_in)
     ]
     results = pl.pallas_call(
-        functools.partial(kernel, dims, span * na * nb, (*semaphores, "first", "second", "third")),
+        functools.partial(kernel, dims, span * na * nb, (*semaphores, "first", "second")),
         out_shape=(
             jax.ShapeDtypeStruct((d_len, span), jnp.bfloat16),
             jax.ShapeDtypeStruct((modes, chans), F32),
@@ -579,7 +570,7 @@
             pltpu.VMEM((nzl, 3, chans, d_len), jnp.bfloat16),
         ]
         + [pltpu.SemaphoreType.DMA((count,)) for count in semaphores.values()]
-        + [pltpu.SemaphoreType.REGULAR] * 3,
+        + [pltpu.SemaphoreType.REGULAR] * 2,
         compiler_params=pltpu.CompilerParams(
             collective_id=0, has_side_effects=True, vmem_limit_bytes=40 * 1024 * 1024
         ),

time: 39.3 us -> 37.7 us (0.959)
  the two profiles are of different devices: /device:TPU:73 before, /device:TPU:480 now
where the time goes in v5:
time: 37.7 us; the launch traced here: 37.4 us
  Pallas kernels  36.8 us (98%)
  between operations  0.64 us (2%)
    pallas_call x1, Pallas kernels, per_device(): pl.pallas_call(functools.partial(kernel, dims, span * na * nb, (*semaphor...  36.1 us

profile of v5, /device:TPU:480, one launch (start us, length us, event | category | flops | bytes accessed | tf_op | source)
XLA Modules:
  0.0 37.4 jit_solution(14633751999958657942)
XLA Ops:
  0.6 36.1 %shard_map.94 = (bf16[1024,128]{1,0:T(8,128)(2,1)S(1)}, f32[16,32]{1,0:T(8,128)S(1)}, f32[16,32]{1,0:T(8,128)S(1)}) custom-call(bf16[32,128]{1,0:T(8,128)(2,1)} %refs_0_.1, bf16[32,128]{1,0:T(8,128)(2,1)} %refs_1_.1, bf16[32,128]{1,0:T(8,128)(2,1)} %refs_2_.1, bf16[32,128]{1,0:T(8,128)(2,1)} %refs_3_.1, f32[16,32]{1,0:T(8,128)} %bitcast.4, ...), custom_call_target="tpu_custom_call" | custom-call | flops 201326592 | bytes 1572864 | tf_op jit(solution)/shard_map/pallas_call | solution.py:552
  36.7 0.7 %shard_map.95 = (bf16[1024,128]{1,0:T(8,128)(2,1)}, f32[16,32]{1,0:T(8,128)}, f32[16,32]{1,0:T(8,128)}) custom-call(bf16[1024,128]{1,0:T(8,128)(2,1)S(1)} %get-tuple-element.9.out_in, f32[16,32]{1,0:T(8,128)S(1)} %get-tuple-element.10.gres_in, f32[16,32]{1,0:T(8,128)S(1)} %get-tuple-element.11.glog_in), custom_call_target="tpu_custom_call" | custom-call | tf_op jit(solution)/shard_map/pallas_call | solution.py:581

commit v6 on v5

--- a/solution.py
+++ b/solution.py
@@ -366,8 +366,6 @@
     @pl.when(zh == 1)
     def _():
         start(twin_copies)
-        pl.semaphore_wait(sems["second"], count_line((CLOSE + 1, -CLOSE - 1)))
-        start_line()
 
     def chained(pieces, length):
         total = pieces[0]
@@ -388,6 +386,11 @@
     passes = jnp.logical_and(same_half, hands_on)
     crosses = jnp.logical_not(same_half)
     pl.when(jnp.logical_or(passes, jnp.logical_and(crosses, zh == 1)))(tuple_copy.start)
+
+    @pl.when(zh == 1)
+    def _():
+        pl.semaphore_wait(sems["second"], count_line((CLOSE + 1, -CLOSE - 1)))
+        start_line()
 
     two = per_core // 2
     begin = core * per_core
@@ -406,8 +409,17 @@
         w3_copies += same_place(view, "w3", plane_peer, y_peers, i * (ny - 1))
     view = across(begin + two, part_rows(half), columns(lax.rem(x, nx // 2) * ny, ny))
     w3_copies += same_place(view, "w3", plane_peer, x_peers, nx // 2 * (ny - 1))
-    whole = w_buf.at[pl.ds(begin, per_core)]
-    w4_copies = [make(whole, whole, "w4", 0, sibling)]
+    w4_copies = []
+
+    def hand_over(view):
+        w4_copies.append(make(view, view, "w4", len(w4_copies), sibling))
+        w4_copies[-1].start()
+
+    def column_from(py, i):
+        return across(begin, pl.ds(0, 2 * HALF), columns(i * ny + py, 1))
+
+    def rows_from(px):
+        return across(begin + two, part_rows(px // (nx // 2)), columns(lax.rem(px, nx // 2) * ny, ny))
 
     pl.when(core == 0)(own_part.wait)
     pl.when(core != 0)(wz_copies[0].wait_recv)
@@ -416,6 +428,9 @@
     start(kv_copies)
     arrive(w2_copies)
     start(w3_copies)
+    for i in range(nx // 2):
+        hand_over(column_from(y, i))
+    hand_over(rows_from(x))
     arrive(twin_copies)
 
     @pl.when(zh == 0)
@@ -428,7 +443,15 @@
     late_buf[0, 0] = (up_f * conv).astype(jnp.bfloat16)
     late_buf[0, 1] = dmixed.astype(jnp.bfloat16)
     late_copies = [make(late_buf.at[0], late_buf.at[k], "late", k - 1, line_peer(k)) for k in line_ways]
-    start(late_copies)
+
+    @pl.when(zlo < nzl // 2)
+    def _():
+        start(reversed(late_copies))
+
+    @pl.when(zlo >= nzl // 2)
+    def _():
+        start(late_copies)
+
     dz_buf[0, 0] = late_buf[0, 0]
     dz_buf[0, 1] = (dmixed * value_f).astype(jnp.bfloat16)
     dz_buf[0, 2] = (dmixed * key_f).astype(jnp.bfloat16)
@@ -440,8 +463,13 @@
         pass_copy.wait_recv()
         pass_copy.start()
 
-    arrive(w3_copies)
-    start(w4_copies)
+    for index, way in reversed(list(enumerate(y_ways))):
+        for i in range(nx // 2):
+            w3_copies[i * (ny - 1) + index].wait_recv()
+            hand_over(column_from(lax.rem(y - way + ny, ny), i))
+    for index, way in reversed(list(enumerate(x_ways))):
+        w3_copies[nx // 2 * (ny - 1) + index].wait_recv()
+        hand_over(rows_from(lax.rem(x - way + nx, nx)))
 
     def hand_out(way, index):
         return pltpu.make_async_remote_copy(
@@ -466,8 +494,8 @@
 
     arrive(kv_copies)
     arrive(w4_copies)
-    arrive(late_copies)
     for k in line_ways:
+        late_copies[k - 1].wait_recv()
         dmixed_k = late_buf[k, 1].astype(F32)
         dz_buf[k, 0] = late_buf[k, 0]
         dz_buf[k, 1] = (dmixed_k * raw_buf[k, 2].astype(F32)).astype(jnp.bfloat16)
@@ -539,7 +567,7 @@
         "late": nzl - 1,
         "w2": nx + ny - 2,
         "w3": nx // 2 * (ny - 1) + nx - 1,
-        "w4": 1,
+        "w4": nx // 2 * ny + nx,
     }
     semaphores = {"load": 6, "own": 1}
     for name, count in counts.items():

time: 37.7 us -> 37.8 us (level)
  no operation moved by 1% of the time
where the time goes in v6:
time: 37.8 us; the launch traced here: 37.2 us
  Pallas kernels  36.6 us (97%)
  between operations  0.64 us (2%)
    pallas_call x1, Pallas kernels, per_device(): pl.pallas_call(functools.partial(kernel, dims, span * na * nb, (*semaphor...  35.9 us

profile of v6, /device:TPU:480, one launch (start us, length us, event | category | flops | bytes accessed | tf_op | source)
XLA Modules:
  0.0 37.2 jit_solution(4430562309484722)
XLA Ops:
  0.6 35.9 %shard_map.94 = (bf16[1024,128]{1,0:T(8,128)(2,1)S(1)}, f32[16,32]{1,0:T(8,128)S(1)}, f32[16,32]{1,0:T(8,128)S(1)}) custom-call(bf16[32,128]{1,0:T(8,128)(2,1)} %refs_0_.1, bf16[32,128]{1,0:T(8,128)(2,1)} %refs_1_.1, bf16[32,128]{1,0:T(8,128)(2,1)} %refs_2_.1, bf16[32,128]{1,0:T(8,128)(2,1)} %refs_3_.1, f32[16,32]{1,0:T(8,128)} %bitcast.4, ...), custom_call_target="tpu_custom_call" | custom-call | flops 201326592 | bytes 1572864 | tf_op jit(solution)/shard_map/pallas_call | solution.py:580
  36.5 0.7 %shard_map.95 = (bf16[1024,128]{1,0:T(8,128)(2,1)}, f32[16,32]{1,0:T(8,128)}, f32[16,32]{1,0:T(8,128)}) custom-call(bf16[1024,128]{1,0:T(8,128)(2,1)S(1)} %get-tuple-element.9.out_in, f32[16,32]{1,0:T(8,128)S(1)} %get-tuple-element.10.gres_in, f32[16,32]{1,0:T(8,128)S(1)} %get-tuple-element.11.glog_in), custom_call_target="tpu_custom_call" | custom-call | tf_op jit(solution)/shard_map/pallas_call | solution.py:609

commit v7 on v5

--- a/solution.py
+++ b/solution.py
@@ -476,7 +476,7 @@
     product = dot(
         dz_buf[...].reshape(rows, span), w_buf[...].reshape(rows, d_len), ((0,), (0,)), None
     )
-    out_ref[...] = product.T.astype(jnp.bfloat16)
+    out_ref[...] = product.astype(jnp.bfloat16).T
 
     pl.when(hands_on)(total_copies[0].wait_recv)
     total = total_buf[...]

time: 37.7 us -> 37.7 us (level)
  no operation moved by 1% of the time
where the time goes in v7:
time: 37.7 us; the launch traced here: 37.4 us
  Pallas kernels  36.8 us (98%)
  between operations  0.64 us (2%)
    pallas_call x1, Pallas kernels, per_device(): pl.pallas_call(functools.partial(kernel, dims, span * na * nb, (*semaphor...  36.1 us

profile of v7, /device:TPU:480, one launch (start us, length us, event | category | flops | bytes accessed | tf_op | source)
XLA Modules:
  0.0 37.4 jit_solution(14981483875927531770)
XLA Ops:
  0.6 36.1 %shard_map.94 = (bf16[1024,128]{1,0:T(8,128)(2,1)S(1)}, f32[16,32]{1,0:T(8,128)S(1)}, f32[16,32]{1,0:T(8,128)S(1)}) custom-call(bf16[32,128]{1,0:T(8,128)(2,1)} %refs_0_.1, bf16[32,128]{1,0:T(8,128)(2,1)} %refs_1_.1, bf16[32,128]{1,0:T(8,128)(2,1)} %refs_2_.1, bf16[32,128]{1,0:T(8,128)(2,1)} %refs_3_.1, f32[16,32]{1,0:T(8,128)} %bitcast.4, ...), custom_call_target="tpu_custom_call" | custom-call | flops 201326592 | bytes 1572864 | tf_op jit(solution)/shard_map/pallas_call | solution.py:552
  36.7 0.7 %shard_map.95 = (bf16[1024,128]{1,0:T(8,128)(2,1)}, f32[16,32]{1,0:T(8,128)}, f32[16,32]{1,0:T(8,128)}) custom-call(bf16[1024,128]{1,0:T(8,128)(2,1)S(1)} %get-tuple-element.9.out_in, f32[16,32]{1,0:T(8,128)S(1)} %get-tuple-element.10.gres_in, f32[16,32]{1,0:T(8,128)S(1)} %get-tuple-element.11.glog_in), custom_call_target="tpu_custom_call" | custom-call | tf_op jit(solution)/shard_map/pallas_call | solution.py:581
